TPU v7x, 32 devices: a whole 2x2x4 slice. The times are simulated.
32 devices in a mesh: row: 8 (over y, x, core), col: 4 (over z).
Axes of the slice: x: 2, y: 2, z: 4, core: 2. Of those that a mesh axis runs over, the one named last changes fastest.
Arguments:
- object_field: float32 [2, 4096, 2048], P(None, 'row', 'col'), may hold values from -6 to 6
- probe: bfloat16 [2, 4, 256, 256], replicated, may hold values from -3 to 3
- patterns: float32 [256, 256, 256], P(('row', 'col')), may hold values from 0.3 to 4
- offsets: int32 [2, 256], P(None, ('row', 'col')), may hold values from 0 to 3840, as said below
- counts: int32 [8, 4], P('row', 'col'), may hold values from 1 to 8, as said below
Outputs:
- object_grad: float32 [2, 4096, 2048], P(None, 'row', 'col')
- probe_grad: float32 [2, 4, 256, 256], replicated
Inputs may be any that keep to these rules, and one draw needn't show every extreme that they name: `offsets`: the patch of a slot held by the device at (r, c) lies inside object rows r * 512 - 128 to (r + 1) * 512 + 128 and columns c * 512 - 128 to (c + 1) * 512 + 128, and inside the object. `counts`: some device has all 8 slots live.
All inputs are finite; a program needn't handle non-finite values.
Results may differ from a plain program's by a relative error of at most 0.005.
Values sent between devices are 32-bit elements; how exact they have to be, the bound alone decides.
A program may use at most 128 MiB of HBM per device.

v0:
```python
import math

import jax
import jax.numpy as jnp
from jax import lax
from jax.sharding import PartitionSpec as P


def shifted(block, axis, distance):
    devices = range(lax.axis_size(axis))
    route = [(i - distance, i) for i in devices if i - distance in devices]
    return lax.ppermute(block, axis, route)


def extended_2(block, sides, width):
    for axis, dim in sides:
        count = lax.axis_size(axis)
        forward = [(i, i + 1) for i in range(count - 1)]
        backward = [(target, source) for source, target in forward]
        low = lax.ppermute(
            lax.slice_in_dim(block, block.shape[dim] - width, None, axis=dim), axis, forward
        )
        high = lax.ppermute(lax.slice_in_dim(block, 0, width, axis=dim), axis, backward)
        block = jnp.concatenate([low, block, high], axis=dim)
    return block


def tables(length):
    index = jnp.arange(length, dtype=jnp.int32)
    product = index[:, None] * index[None, :] % length
    angle = product.astype(jnp.float32) * (2.0 * math.pi / length)
    factor = 1.0 / math.sqrt(length)
    return (
        (jnp.cos(angle) * factor).astype(jnp.bfloat16),
        (-jnp.sin(angle) * factor).astype(jnp.bfloat16),
    )


def right_dot(matrix, table):
    return jnp.einsum("kab,bc->kac", matrix, table, preferred_element_type=jnp.float32)


def left_dot(table, matrix):
    return jnp.einsum("ab,kbc->kac", table, matrix, preferred_element_type=jnp.float32)


def right_mult(real_part, imag_part, table_re, table_im):
    return (
        right_dot(real_part, table_re) - right_dot(imag_part, table_im),
        right_dot(real_part, table_im) + right_dot(imag_part, table_re),
    )


def left_mult(table_re, table_im, real_part, imag_part):
    return (
        left_dot(table_re, real_part) - left_dot(table_im, imag_part),
        left_dot(table_re, imag_part) + left_dot(table_im, real_part),
    )


def position(patch_re, patch_im, measured, probe_re, probe_im, table_re, table_im):
    probe_fr = probe_re.astype(jnp.float32)
    probe_fi = probe_im.astype(jnp.float32)
    exit_re = (probe_fr * patch_re - probe_fi * patch_im).astype(jnp.bfloat16)
    exit_im = (probe_fr * patch_im + probe_fi * patch_re).astype(jnp.bfloat16)
    half_re, half_im = right_mult(exit_re, exit_im, table_re, table_im)
    field_re, field_im = left_mult(
        table_re, table_im, half_re.astype(jnp.bfloat16), half_im.astype(jnp.bfloat16)
    )
    intensity = jnp.sum(field_re * field_re + field_im * field_im, axis=0)
    amplitude = jnp.sqrt(jnp.maximum(intensity, 1.0))
    ratio = 1.0 - measured / amplitude
    resid_re = (field_re * ratio).astype(jnp.bfloat16)
    resid_im = (field_im * ratio).astype(jnp.bfloat16)
    conj_im = -table_im
    back_re, back_im = right_mult(resid_re, resid_im, table_re, conj_im)
    wave_re, wave_im = left_mult(
        table_re, conj_im, back_re.astype(jnp.bfloat16), back_im.astype(jnp.bfloat16)
    )
    object_re = jnp.sum(probe_fr * wave_re + probe_fi * wave_im, axis=0)
    object_im = jnp.sum(probe_fr * wave_im - probe_fi * wave_re, axis=0)
    update_re = patch_re * wave_re + patch_im * wave_im
    update_im = patch_re * wave_im - patch_im * wave_re
    return (jnp.stack([object_re, object_im]), jnp.stack([update_re, update_im]))


def send_cols(strip, amount):
    return shifted(strip, "col", amount)


def send_rows(strip, amount):
    return shifted(strip, "row", amount)


def on_device(object_field, probe, patterns, offsets, counts):
    tile_rows = object_field.shape[1]
    tile_cols = object_field.shape[2]
    slots = patterns.shape[0]
    width = patterns.shape[1]
    margin = width // 2
    modes = probe.shape[1]
    zero_index = jnp.int32(0)
    extended = extended_2(object_field, (("row", 1), ("col", 2)), margin)
    base_row = lax.axis_index("row") * tile_rows - margin
    base_col = lax.axis_index("col") * tile_cols - margin
    local_rows = offsets[0] - base_row
    local_cols = offsets[1] - base_col
    alive = jnp.arange(slots, dtype=jnp.int32) < counts[0, 0]
    table_re, table_im = tables(width)
    probe_re = probe[0]
    probe_im = probe[1]

    def cut_patch(start_row, start_col):
        return lax.dynamic_slice(extended, (zero_index, start_row, start_col), (2, width, width))

    def add_patch(totals, term, start_row, start_col):
        previous = lax.dynamic_slice(totals, (zero_index, start_row, start_col), (2, width, width))
        return lax.dynamic_update_slice(totals, previous + term, (zero_index, start_row, start_col))

    empty_ext = jnp.zeros(extended.shape, jnp.float32)
    empty_probe = jnp.zeros((2, modes, width, width), jnp.float32)

    def visit(number, carried):

        def work(inner):
            totals, probe_total = inner
            patch = cut_patch(local_rows[number], local_cols[number])
            object_term, probe_term = position(
                patch[0], patch[1], patterns[number], probe_re, probe_im, table_re, table_im
            )
            totals = add_patch(totals, object_term, local_rows[number], local_cols[number])
            return (totals, probe_total + probe_term)

        return lax.cond(alive[number], work, lambda inner: inner, carried)

    totals, probe_total = lax.fori_loop(0, slots, visit, (empty_ext, empty_probe))
    from_left = send_cols(totals[:, :, tile_cols + margin :], 1)
    from_right = send_cols(totals[:, :, :margin], -1)
    totals = totals.at[:, :, margin : 2 * margin].add(from_left)
    totals = totals.at[:, :, tile_cols : tile_cols + margin].add(from_right)
    from_above = send_rows(totals[:, tile_rows + margin :, margin : margin + tile_cols], 1)
    from_below = send_rows(totals[:, :margin, margin : margin + tile_cols], -1)
    totals = totals.at[:, margin : 2 * margin, margin : margin + tile_cols].add(from_above)
    totals = totals.at[:, tile_rows : tile_rows + margin, margin : margin + tile_cols].add(
        from_below
    )
    object_grad = totals[:, margin : margin + tile_rows, margin : margin + tile_cols]
    probe_grad = lax.psum(probe_total, ("row", "col"))
    return (object_grad, probe_grad)


def solution(mesh):
    in_specs = (
        P(None, "row", "col"),
        P(),
        P(("row", "col"), None, None),
        P(None, ("row", "col")),
        P("row", "col"),
    )
    out_specs = (P(None, "row", "col"), P())
    return jax.shard_map(
        on_device, mesh=mesh, in_specs=in_specs, out_specs=out_specs, check_vma=False
    )
```

profile of v0, /device:TPU:0, one launch (start us, length us, event | category | flops | bytes accessed | tf_op | source)
XLA Modules:
  0.0 430.3 jit_solution(15001151872987375030)
XLA Ops:
  7.2 1.9 copy.47
  9.2 2.4 collective-permute-start
  11.6 1.3 collective-permute-start.1
  13.1 4.4 %collective-permute-done.1 = f32[2,128,512]{1,2,0:T(8,128)S(1)} collective-permute-done((f32[2,128,512]{1,2,0:T(8,128)S(1)}, f32[2,128,512]{1,2,0:T(8,128)S(1)}, u32[]{:S(2)}, u32[]{:S(2)}) %collective-permute-start.1) | collective-permute-done | bytes 524320 | tf_op jit(solution)/shard_map/ppermute | solution.py:23
  17.5 1.3 pad_maximum_fusion.3
  18.8 4.5 %collective-permute-start.2 = (f32[2,768,128]{1,2,0:T(8,128)}, f32[2,768,128]{1,2,0:T(8,128)}, u32[]{:S(2)}, u32[]{:S(2)}) collective-permute-start(f32[2,768,128]{1,2,0:T(8,128)} %get-tuple-element.491), channel_id=1, source_target_pairs={{0,1},{1,2},{2,3},{4,5},{5,6},{6,7},{8,9},{9,10},{10,11},{12,13},{... | collective-permute-start | bytes 2359304 | tf_op jit(solution)/shard_map/ppermute | solution.py:20
  23.3 1.3 collective-permute-start.3
  24.6 2.3 fusion.67
  26.9 1.2 copy.73
  28.2 1.2 copy.74
  29.4 2.9 copy.51
  33.0 4.5 %collective-permute-done.3 = f32[2,768,128]{1,2,0:T(8,128)} collective-permute-done((f32[2,768,128]{1,2,0:T(8,128)}, f32[2,768,128]{1,2,0:T(8,128)}, u32[]{:S(2)}, u32[]{:S(2)}) %collective-permute-start.3) | collective-permute-done | bytes 786464 | tf_op jit(solution)/shard_map/ppermute | solution.py:23
  37.5 3.6 pad_maximum_fusion
  41.1 2.5 broadcast_in_dim.4
  43.8 66.5 %while.21 = (s32[]{:T(128)}, f32[2,768,768]{1,2,0:T(8,128)}, f32[2,4,256,256]{2,3,1,0:T(8,128)S(1)}, pred[8]{0:T(512)(128)(4,1)S(1)}, s32[8]{0:T(128)S(1)}, /*in...) while((s32[]{:T(128)}, f32[2,768,768]{1,2,0:T(8,128)}, ...), condition=%wide.region_6.7_spmd.clone.clone, body=%wide.region_0.6_spmd.clone.clone.sunk | while | flops 2167078912 | bytes 57410060 | solution.py:136
  43.8 1.1 multiply_convert_fusion.9
  44.9 0.6 dynamic_slice.29
  46.1 23.7 %conditional.4 = ((f32[2,768,768]{1,2,0:T(8,128)}, f32[2,4,256,256]{2,3,1,0:T(8,128)S(1)})) conditional(s32[]{:T(128)} %bitcast.99, (f32[2,768,768]{1,2,0:T(8,128)}, f32[2,4,256,256]{2,3,1,0:T(8,128)S(1)}) %tuple.84, (s32[]{:T(128)}, s32[8]{0:T(128)S(1)}, s32[8]{0:T(128)S(1)}, f32[2,768,768]{1,2,0:T(8,128)}, bf16[4,256,256]{1,2,0:T(8,128)(2,1)S(1)}, ...), branch_computations={%region_1.1_spmd, %region_2.5_spmd} | conditional | flops 2165833728 | bytes 57147580 | solution.py:134
  46.2 0.6 dynamic_slice.19
  48.7 0.6 dynamic_slice.18
  51.2 1.3 dynamic-slice_bitcast_fusion.1
  56.0 1.0 fusion.21
  59.5 0.9 add_bitcast_fusion
  60.9 2.2 maximum_add_fusion.1
  63.1 6.7 %dynamic_update_slice.2 = f32[2,768,768]{1,2,0:T(8,128)} dynamic-update-slice(f32[2,768,768]{1,2,0:T(8,128)} %get-tuple-element.305, f32[2,256,256]{1,2,0:T(8,128)} %maximum_add_fusion.1, s32[]{:T(128)} %constant.165.clone, s32[]{:T(128)S(6)} %select_n.41, s32[]{:T(128)S(6)} %select_n.42) | dynamic-update-slice | bytes 1048580 | tf_op jit(solution)/shard_map/while/body/eval_jaxpr/cond/branch_1_fun/dynamic_update_slice | solution.py:118
  69.8 1.1 multiply_convert_fusion.9
  70.9 0.6 dynamic_slice.29
  72.2 23.7 %conditional.4 = ((f32[2,768,768]{1,2,0:T(8,128)}, f32[2,4,256,256]{2,3,1,0:T(8,128)S(1)})) conditional(s32[]{:T(128)} %bitcast.99, (f32[2,768,768]{1,2,0:T(8,128)}, f32[2,4,256,256]{2,3,1,0:T(8,128)S(1)}) %tuple.84, (s32[]{:T(128)}, s32[8]{0:T(128)S(1)}, s32[8]{0:T(128)S(1)}, f32[2,768,768]{1,2,0:T(8,128)}, bf16[4,256,256]{1,2,0:T(8,128)(2,1)S(1)}, ...), branch_computations={%region_1.1_spmd, %region_2.5_spmd} | conditional | flops 2165833728 | bytes 57147580 | solution.py:134
  74.7 0.6 dynamic_slice.18
  77.2 1.3 dynamic-slice_bitcast_fusion.1
  82.0 1.0 fusion.21
  85.5 0.9 add_bitcast_fusion
  86.9 2.2 maximum_add_fusion.1
  89.1 6.8 %dynamic_update_slice.2 = f32[2,768,768]{1,2,0:T(8,128)} dynamic-update-slice(f32[2,768,768]{1,2,0:T(8,128)} %get-tuple-element.305, f32[2,256,256]{1,2,0:T(8,128)} %maximum_add_fusion.1, s32[]{:T(128)} %constant.165.clone, s32[]{:T(128)S(6)} %select_n.41, s32[]{:T(128)S(6)} %select_n.42) | dynamic-update-slice | bytes 1048580 | tf_op jit(solution)/shard_map/while/body/eval_jaxpr/cond/branch_1_fun/dynamic_update_slice | solution.py:118
  95.9 1.1 multiply_convert_fusion.9
  97.0 0.6 dynamic_slice.29
  98.3 1.1 multiply_convert_fusion.9
  99.4 0.6 dynamic_slice.29
  100.7 1.1 multiply_convert_fusion.9
  101.8 0.6 dynamic_slice.29
  103.1 1.1 multiply_convert_fusion.9
  104.2 0.6 dynamic_slice.29
  105.5 1.1 multiply_convert_fusion.9
  106.6 0.6 dynamic_slice.29
  107.9 1.1 multiply_convert_fusion.9
  109.0 0.6 dynamic_slice.29
  110.2 6.1 %copy.54 = f32[2,768,768]{2,1,0:T(8,128)} copy(f32[2,768,768]{1,2,0:T(8,128)} %get-tuple-element.363) | data formatting | bytes 9437184 | tf_op jit(solution)/shard_map/while | solution.py:136
  116.3 1.5 fusion.65
  117.8 46.0 %collective-permute-start.4 = (f32[2,768,128]{2,1,0:T(8,128)S(1)}, f32[2,768,128]{2,1,0:T(8,128)S(1)}, u32[]{:S(2)}, u32[]{:S(2)}) collective-permute-start(f32[2,768,128]{2,1,0:T(8,128)S(1)} %get-tuple-element.490), channel_id=1, source_target_pairs={{0,1},{1,2},{2,3},{4,5},{5,6},{6,7},{8,9},{9,10},{10,11},{12,13},{... | collective-permute-start | bytes 2359304 | tf_op jit(solution)/shard_map/ppermute | solution.py:12
  163.9 1.3 collective-permute-start.5
  165.2 8.1 %collective-permute-done.4 = f32[2,768,128]{2,1,0:T(8,128)S(1)} collective-permute-done((f32[2,768,128]{2,1,0:T(8,128)S(1)}, f32[2,768,128]{2,1,0:T(8,128)S(1)}, u32[]{:S(2)}, u32[]{:S(2)}) %collective-permute-start.4) | collective-permute-done | bytes 786464 | tf_op jit(solution)/shard_map/ppermute | solution.py:12
  173.3 2.2 fusion.61
  175.5 26.7 %collective-permute-done.5 = f32[2,768,128]{2,1,0:T(8,128)S(1)} collective-permute-done((f32[2,768,128]{2,1,0:T(8,128)S(1)}, f32[2,768,128]{2,1,0:T(8,128)S(1)}, u32[]{:S(2)}, u32[]{:S(2)}) %collective-permute-start.5) | collective-permute-done | bytes 786464 | tf_op jit(solution)/shard_map/ppermute | solution.py:12
  202.2 2.2 fusion.60
  204.4 1.1 slice.175
  205.5 1.3 collective-permute-start.6
  206.8 1.8 copy.56
  208.7 2.2 fusion.64
  210.8 1.3 collective-permute-start.7
  212.1 47.5 %collective-permute-done.7 = f32[2,128,512]{2,1,0:T(8,128)S(1)} collective-permute-done((f32[2,128,512]{2,1,0:T(8,128)S(1)}, f32[2,128,512]{2,1,0:T(8,128)S(1)}, u32[]{:S(2)}, u32[]{:S(2)}) %collective-permute-start.7) | collective-permute-done | bytes 524320 | tf_op jit(solution)/shard_map/ppermute | solution.py:12
  259.7 1.9 fusion.62
  261.6 3.1 slice.178
  264.7 155.8 %all-reduce.2.cloned.1.call-done = f32[2,4,256,256]{3,2,1,0:T(8,128)} async-done(((f32[2,4,256,256]{3,2,1,0:T(8,128)}), f32[2,4,256,256]{3,2,1,0:T(8,128)}) %all-reduce.2.cloned.1.call-update) | async-done | bytes 2097168 | tf_op jit(solution)/shard_map/psum | solution.py:148
  420.5 3.0 copy.97
  (54 shorter events, 13.9 us)
Async XLA Ops:
  7.2 413.3 %all-reduce.2.cloned.1.call-start = ((), (), s32[]{:S(2)}) async-start(), calls=%async_computation | async-start | bytes 4194304 | tf_op jit(solution)/shard_map/psum | solution.py:148
  9.2 3.9 collective-permute-start
  11.6 5.9 %collective-permute-start.1 = (f32[2,128,512]{1,2,0:T(8,128)S(1)}, f32[2,128,512]{1,2,0:T(8,128)S(1)}, u32[]{:S(2)}, u32[]{:S(2)}) collective-permute-start(f32[2,128,512]{1,2,0:T(8,128)S(1)} %get-tuple-element.494), channel_id=1, source_target_pairs={{4,0},{8,4},{12,8},{16,12},{20,16},{24,20},{28,24},{5,1},{9,5},{13... | collective-permute-start | bytes 1572872 | tf_op jit(solution)/shard_map/ppermute | solution.py:23
  13.1 13.8 %copy-start = (f32[2,128,512]{1,2,0:T(8,128)}, f32[2,128,512]{1,2,0:T(8,128)S(1)}, u32[]{:S(2)}) copy-start(f32[2,128,512]{1,2,0:T(8,128)S(1)} %collective-permute-done) | copy-start | bytes 1572868
  17.5 10.6 %copy-start.1 = (f32[2,128,512]{1,2,0:T(8,128)}, f32[2,128,512]{1,2,0:T(8,128)S(1)}, u32[]{:S(2)}) copy-start(f32[2,128,512]{1,2,0:T(8,128)S(1)} %collective-permute-done.1) | copy-start | bytes 1572868
  18.8 14.1 %copy-start.2 = (s32[2,8]{1,0:T(2,128)S(1)}, s32[2,8]{1,0:T(2,128)}, u32[]{:S(2)}) copy-start(s32[2,8]{1,0:T(2,128)} %param.20) | copy-start | bytes 196
  18.8 14.1 %collective-permute-start.2 = (f32[2,768,128]{1,2,0:T(8,128)}, f32[2,768,128]{1,2,0:T(8,128)}, u32[]{:S(2)}, u32[]{:S(2)}) collective-permute-start(f32[2,768,128]{1,2,0:T(8,128)} %get-tuple-element.491), channel_id=1, source_target_pairs={{0,1},{1,2},{2,3},{4,5},{5,6},{6,7},{8,9},{9,10},{10,11},{12,13},{... | collective-permute-start | bytes 2359304 | tf_op jit(solution)/shard_map/ppermute | solution.py:20
  23.3 14.2 %collective-permute-start.3 = (f32[2,768,128]{1,2,0:T(8,128)}, f32[2,768,128]{1,2,0:T(8,128)}, u32[]{:S(2)}, u32[]{:S(2)}) collective-permute-start(f32[2,768,128]{1,2,0:T(8,128)} %get-tuple-element.492), channel_id=1, source_target_pairs={{1,0},{2,1},{3,2},{5,4},{6,5},{7,6},{9,8},{10,9},{11,10},{13,12},{... | collective-permute-start | bytes 2359304 | tf_op jit(solution)/shard_map/ppermute | solution.py:23
  117.8 55.5 %collective-permute-start.4 = (f32[2,768,128]{2,1,0:T(8,128)S(1)}, f32[2,768,128]{2,1,0:T(8,128)S(1)}, u32[]{:S(2)}, u32[]{:S(2)}) collective-permute-start(f32[2,768,128]{2,1,0:T(8,128)S(1)} %get-tuple-element.490), channel_id=1, source_target_pairs={{0,1},{1,2},{2,3},{4,5},{5,6},{6,7},{8,9},{9,10},{10,11},{12,13},{... | collective-permute-start | bytes 2359304 | tf_op jit(solution)/shard_map/ppermute | solution.py:12
  163.9 38.3 %collective-permute-start.5 = (f32[2,768,128]{2,1,0:T(8,128)S(1)}, f32[2,768,128]{2,1,0:T(8,128)S(1)}, u32[]{:S(2)}, u32[]{:S(2)}) collective-permute-start(f32[2,768,128]{2,1,0:T(8,128)S(1)} %get-tuple-element.489), channel_id=1, source_target_pairs={{1,0},{2,1},{3,2},{5,4},{6,5},{7,6},{9,8},{10,9},{11,10},{13,12},{... | collective-permute-start | bytes 2359304 | tf_op jit(solution)/shard_map/ppermute | solution.py:12
  205.5 3.2 collective-permute-start.6
  210.8 48.8 %collective-permute-start.7 = (f32[2,128,512]{2,1,0:T(8,128)S(1)}, f32[2,128,512]{2,1,0:T(8,128)S(1)}, u32[]{:S(2)}, u32[]{:S(2)}) collective-permute-start(f32[2,128,512]{2,1,0:T(8,128)S(1)} %get-tuple-element.487), channel_id=1, source_target_pairs={{4,0},{8,4},{12,8},{16,12},{20,16},{24,20},{28,24},{5,1},{9,5},{13... | collective-permute-start | bytes 1572872 | tf_op jit(solution)/shard_map/ppermute | solution.py:12
Sparse Core Ops, SparseCore 0:
  208.8 211.6 all-reduce.1
where the time goes:
time: 436 us; the launch traced here: 430 us
  waiting for transfers between devices  247 us (57%)
  starting transfers between devices  59.4 us (14%)
  local copies, waits for them, and re-layouts  52.2 us (12%)
  other arithmetic  29.7 us (7%)
  between operations  14.8 us (3%)
  loops' own time  13.6 us (3%)
  matrix products  13.3 us (3%)
    psum x1, waiting for transfers between devices, on_device(): probe_grad = lax.psum(probe_total, ('row', 'col'))  156 us
    ppermute x4, waiting for transfers between devices, shifted(): return lax.ppermute(block, axis, route)  82.4 us
    ppermute x4, starting transfers between devices, shifted(): return lax.ppermute(block, axis, route)  49.9 us
    dynamic_update_slice x2, local copies, waits for them, and re-layouts, add_patch(): lax.dynamic_update_slice(totals, previous + term, (zero_index, start_row,...  13.5 us
    unnamed x11, local copies, waits for them, and re-layouts  10.4 us
    ppermute x2, waiting for transfers between devices, extended_2(): lax.ppermute(lax.slice_in_dim(block, 0, width, axis=dim), axis, backward)  8.93 us
    convert_element_type x8, other arithmetic, tables(): (-jnp.sin(angle) * factor).astype(jnp.bfloat16)  8.85 us
  transfers between devices with their start and end apart: 9, of which 7 were waited for; matrix products, arithmetic and copies ran while one was open for 4% of the time, Pallas kernels for 0%

commit v1 on v0

v1 whole, which is shorter than its diff:
```python
import math

import jax
import jax.numpy as jnp
import ml_dtypes
import numpy as np
from jax import lax
from jax.experimental import pallas as pl
from jax.experimental.pallas import tpu as pltpu
from jax.sharding import PartitionSpec as P

F32 = jnp.float32
BF16 = jnp.bfloat16


def shifted(block, axis, distance):
    devices = range(lax.axis_size(axis))
    route = [(i - distance, i) for i in devices if i - distance in devices]
    return lax.ppermute(block, axis, route)


def tables(length):
    index = np.arange(length)
    product = index[:, None] * index[None, :] % length
    angle = product.astype(np.float32) * np.float32(2.0 * math.pi / length)
    factor = np.float32(1.0 / math.sqrt(length))
    re = (np.cos(angle) * factor).astype(ml_dtypes.bfloat16)
    im = (-np.sin(angle) * factor).astype(ml_dtypes.bfloat16)
    half = length // 2
    right = []
    left = []
    for parity in range(2):
        a, b = re[:half, parity::2], im[:half, parity::2]
        right.append(np.block([[a, b], [-b, a]]))
        a, b = re[parity::2, :half], im[parity::2, :half]
        left.append(np.block([[a, -b], [b, a]]))
    order = np.concatenate([index[0::2], index[1::2]])
    spread = (index[:, None] == order[None, :]).astype(ml_dtypes.bfloat16)
    return np.stack(right + left + [spread])


def mm(a, b):
    return jnp.dot(a, b, preferred_element_type=F32)


SUB = 8
LANES = 128


def rows_up(block, shift):
    tiles = block.reshape(-1, SUB, LANES)
    tiles = pltpu.roll(tiles, lax.rem(SUB - shift, SUB), 1)
    near = lax.broadcasted_iota(jnp.int32, (1, SUB, LANES), 1) < SUB - shift
    return jnp.where(near, tiles[:-1], tiles[1:]).reshape(-1, LANES)


def rows_down(block, shift):
    tiles = pltpu.roll(block.reshape(-1, SUB, LANES), lax.rem(shift, SUB), 1)
    near = lax.broadcasted_iota(jnp.int32, (1, SUB, LANES), 1) >= shift
    zero = jnp.zeros((1, SUB, LANES), F32)
    high = jnp.concatenate([tiles, zero], axis=0)
    low = jnp.concatenate([zero, tiles], axis=0)
    return jnp.where(near, high, low).reshape(-1, LANES)


def kernel(
    rows_ref, cols_ref, count_ref,
    object_ref, left_ref, right_ref, top_ref, bottom_ref, probe_ref, pattern_lo, pattern_hi, table_ref,
    up_ref, middle_ref, down_ref, update_ref,
    ext, totals, patch, field, residual, term, sems,
):
    number = pl.program_id(0)
    last = pl.num_programs(0) - 1
    tile_rows, tile_cols = object_ref.shape[1:]
    margin = top_ref.shape[1]
    modes, width = probe_ref.shape[1:3]
    half = width // 2
    lanes = LANES

    @pl.when(number == 0)
    def _():
        body = pl.ds(margin, tile_rows)
        copies = [
            pltpu.make_async_copy(object_ref, ext.at[:, body, pl.ds(margin, tile_cols)], sems.at[0]),
            pltpu.make_async_copy(left_ref, ext.at[:, body, pl.ds(0, margin)], sems.at[1]),
            pltpu.make_async_copy(
                right_ref, ext.at[:, body, pl.ds(margin + tile_cols, margin)], sems.at[2]
            ),
            pltpu.make_async_copy(top_ref, ext.at[:, pl.ds(0, margin), :], sems.at[3]),
            pltpu.make_async_copy(
                bottom_ref, ext.at[:, pl.ds(margin + tile_rows, margin), :], sems.at[4]
            ),
        ]
        for copy in copies:
            copy.start()
        totals[...] = jnp.zeros_like(totals)
        update_ref[...] = jnp.zeros_like(update_ref)
        for copy in copies:
            copy.wait()

    @pl.when(number < count_ref[0])
    def _():
        row = rows_ref[number]
        col = cols_ref[number]
        limit = ext.shape[2] - width - lanes
        base = pl.multiple_of(jnp.minimum(col // lanes * lanes, limit), lanes)
        shift = col - base
        tall = width + SUB
        row_base = pl.multiple_of(jnp.minimum(row // SUB * SUB, ext.shape[1] - tall), SUB)
        row_shift = row - row_base
        lane = lax.broadcasted_iota(jnp.int32, (width, lanes), 1)
        back = lax.rem(lanes - shift, lanes)
        ahead = lax.rem(shift, lanes)
        near = lane < lanes - shift
        for part in range(2):
            pieces = [
                pltpu.roll(
                    rows_up(
                        ext[part, pl.ds(row_base, tall), pl.ds(base + t * lanes, lanes)], row_shift
                    ),
                    back,
                    1,
                )
                for t in range(width // lanes + 1)
            ]
            for t in range(width // lanes):
                patch[part, :, t * lanes : (t + 1) * lanes] = jnp.where(
                    near, pieces[t], pieces[t + 1]
                )

        r_even, r_odd = table_ref[0], table_ref[1]
        l_even, l_odd = table_ref[2], table_ref[3]
        spread = table_ref[4]

        intensity = [jnp.zeros((half, width), F32) for _ in range(2)]
        for k in range(modes):
            o_re, o_im = patch[0], patch[1]
            p_re = probe_ref[0, k].astype(F32)
            p_im = probe_ref[1, k].astype(F32)
            x_re = p_re * o_re - p_im * o_im
            x_im = p_re * o_im + p_im * o_re
            s = jnp.concatenate(
                [x_re[:, :half] + x_re[:, half:], x_im[:, :half] + x_im[:, half:]], axis=1
            ).astype(BF16)
            d = jnp.concatenate(
                [x_re[:, :half] - x_re[:, half:], x_im[:, :half] - x_im[:, half:]], axis=1
            ).astype(BF16)
            y_even = mm(s, r_even)
            y_odd = mm(d, r_odd)
            for parity, table in enumerate((l_even, l_odd)):
                if parity == 0:
                    a = y_even[:half] + y_even[half:]
                    b = y_odd[:half] + y_odd[half:]
                else:
                    a = y_even[:half] - y_even[half:]
                    b = y_odd[:half] - y_odd[half:]
                u = jnp.concatenate(
                    [
                        jnp.concatenate([a[:, :half], b[:, :half]], axis=1),
                        jnp.concatenate([a[:, half:], b[:, half:]], axis=1),
                    ],
                    axis=0,
                ).astype(BF16)
                f = mm(table, u)
                field[k, parity] = f
                intensity[parity] += f[:half] * f[:half] + f[half:] * f[half:]

        for parity in range(2):
            rows_of = (0, pl.ds(parity, half, 2), slice(None))
            measured = jnp.concatenate([pattern_lo[rows_of], pattern_hi[rows_of]], axis=1)
            coarse = measured.astype(BF16)
            fine = (measured - coarse.astype(F32)).astype(BF16)
            measured = mm(coarse, spread) + mm(fine, spread)
            ratio = 1.0 - measured * lax.rsqrt(jnp.maximum(intensity[parity], 1.0))
            here = slice(parity * half, (parity + 1) * half)
            for k in range(modes):
                c_re = (field[k, parity, :half] * ratio).astype(BF16)
                c_im = (field[k, parity, half:] * ratio).astype(BF16)
                residual[k, 0, here, :half] = c_re[:, :half]
                residual[k, 0, here, half:] = c_im[:, :half]
                residual[k, 1, here, :half] = c_re[:, half:]
                residual[k, 1, here, half:] = c_im[:, half:]

        for k in range(modes):
            g_even = mm(residual[k, 0], l_even)
            g_odd = mm(residual[k, 1], l_odd)
            a = g_even + g_odd
            b = g_even - g_odd
            waves = []
            for parity, table in enumerate((r_even, r_odd)):
                here = slice(parity * half, (parity + 1) * half)
                v = jnp.concatenate(
                    [
                        jnp.concatenate([a[here, :half], b[here, :half]], axis=1),
                        jnp.concatenate([a[here, half:], b[here, half:]], axis=1),
                    ],
                    axis=0,
                ).astype(BF16)
                waves.append(mm(table, v))
            for part in range(2):
                wave = waves[0] + waves[1] if part == 0 else waves[0] - waves[1]
                w_re, w_im = wave[:half], wave[half:]
                here = slice(part * half, (part + 1) * half)
                p_re = probe_ref[0, k, here].astype(F32)
                p_im = probe_ref[1, k, here].astype(F32)
                o_re, o_im = patch[0, here], patch[1, here]
                t_re = p_re * w_re + p_im * w_im
                t_im = p_re * w_im - p_im * w_re
                if k == 0:
                    term[0, here] = t_re
                    term[1, here] = t_im
                else:
                    term[0, here] += t_re
                    term[1, here] += t_im
                update_ref[0, k, here] += o_re * w_re + o_im * w_im
                update_ref[1, k, here] += o_re * w_im - o_im * w_re

        far = lane >= shift
        for part in range(2):
            pieces = [
                pltpu.roll(term[part, :, t * lanes : (t + 1) * lanes], ahead, 1)
                for t in range(width // lanes)
            ]
            for t in range(width // lanes + 1):
                low = pieces[t - 1] if t > 0 else 0.0
                high = pieces[t] if t < width // lanes else 0.0
                where = (part, pl.ds(row_base, tall), pl.ds(base + t * lanes, lanes))
                totals[where] += rows_down(jnp.where(far, high, low), row_shift)

    @pl.when(number == last)
    def _():
        copies = [
            pltpu.make_async_copy(totals.at[:, pl.ds(0, margin), :], up_ref, sems.at[0]),
            pltpu.make_async_copy(totals.at[:, pl.ds(margin, tile_rows), :], middle_ref, sems.at[1]),
            pltpu.make_async_copy(
                totals.at[:, pl.ds(margin + tile_rows, margin), :], down_ref, sems.at[2]
            ),
        ]
        for copy in copies:
            copy.start()
        for copy in copies:
            copy.wait()


def gradients(rows, cols, count, object_field, left, right, top, bottom, probe, patterns, table):
    slots, width = patterns.shape[:2]
    modes = probe.shape[1]
    tile_rows, tile_cols = object_field.shape[1:]
    margin = width // 2
    full = (2, tile_rows + 2 * margin, tile_cols + 2 * margin)
    anywhere = pl.BlockSpec(memory_space=pl.ANY)

    def whole(shape):
        return pl.BlockSpec(shape, lambda n, *_: (0,) * len(shape))

    flops = slots * modes * 8 * 2 * width**3
    return pl.pallas_call(
        kernel,
        grid_spec=pltpu.PrefetchScalarGridSpec(
            num_scalar_prefetch=3,
            grid=(slots,),
            in_specs=[anywhere] * 5
            + [
                whole(probe.shape),
                pl.BlockSpec((1, width, width // 2), lambda n, *_: (n, 0, 0)),
                pl.BlockSpec((1, width, width // 2), lambda n, *_: (n, 0, 1)),
                whole(table.shape),
            ],
            out_specs=[anywhere] * 3 + [whole(probe.shape)],
            scratch_shapes=[
                pltpu.VMEM(full, F32),
                pltpu.VMEM(full, F32),
                pltpu.VMEM((2, width, width), F32),
                pltpu.VMEM((modes, 2, width, width), F32),
                pltpu.VMEM((modes, 2, width, width), BF16),
                pltpu.VMEM((2, width, width), F32),
                pltpu.SemaphoreType.DMA((5,)),
            ],
        ),
        out_shape=[
            jax.ShapeDtypeStruct((2, margin, full[2]), F32),
            jax.ShapeDtypeStruct((2, tile_rows, full[2]), F32),
            jax.ShapeDtypeStruct((2, margin, full[2]), F32),
            jax.ShapeDtypeStruct(probe.shape, F32),
        ],
        compiler_params=pltpu.CompilerParams(vmem_limit_bytes=56 * 2**20),
        cost_estimate=pl.CostEstimate(
            flops=flops, bytes_accessed=16 * 2**20, transcendentals=slots * width * width
        ),
    )(rows, cols, count, object_field, left, right, top, bottom, probe, patterns, patterns, table)


def on_device(object_field, probe, patterns, offsets, counts):
    tile_rows, tile_cols = object_field.shape[1:]
    width = patterns.shape[1]
    margin = width // 2
    base_row = lax.axis_index("row") * tile_rows - margin
    base_col = lax.axis_index("col") * tile_cols - margin
    table = jnp.asarray(tables(width))

    left = shifted(object_field[:, :, tile_cols - margin :], "col", 1)
    right = shifted(object_field[:, :, :margin], "col", -1)
    tail = slice(tile_rows - margin, None)
    head = slice(None, margin)
    lower = jnp.concatenate([left[:, tail], object_field[:, tail], right[:, tail]], axis=2)
    upper = jnp.concatenate([left[:, head], object_field[:, head], right[:, head]], axis=2)
    top = shifted(lower, "row", 1)
    bottom = shifted(upper, "row", -1)

    up, middle, down, update = gradients(
        offsets[0] - base_row, offsets[1] - base_col, counts.reshape(-1),
        object_field, left, right, top, bottom, probe, patterns, table,
    )
    probe_grad = lax.psum(update, ("row", "col"))
    from_above = shifted(down, "row", 1)
    from_below = shifted(up, "row", -1)
    middle = middle.at[:, head].add(from_above).at[:, tail].add(from_below)
    from_left = shifted(middle[:, :, tile_cols + margin :], "col", 1)
    from_right = shifted(middle[:, :, :margin], "col", -1)
    object_grad = middle[:, :, margin : margin + tile_cols]
    object_grad = object_grad.at[:, :, :margin].add(from_left)
    object_grad = object_grad.at[:, :, tile_cols - margin :].add(from_right)
    return (object_grad, probe_grad)


def solution(mesh):
    in_specs = (
        P(None, "row", "col"),
        P(),
        P(("row", "col"), None, None),
        P(None, ("row", "col")),
        P("row", "col"),
    )
    out_specs = (P(None, "row", "col"), P())
    return jax.shard_map(
        on_device, mesh=mesh, in_specs=in_specs, out_specs=out_specs, check_vma=False
    )
```

time: 436 us -> 250 us (0.57); the launches traced: 430 us -> 250 us
  waiting for transfers between devices: 247 us -> 169 us
  local copies, waits for them, and re-layouts: 52.2 us -> 8.61 us
  starting transfers between devices: 59.4 us -> 26.6 us
  Pallas kernels: 0 us -> 21.7 us
  other arithmetic: 29.7 us -> 8.69 us
  loops' own time: 13.6 us -> 0 us
  matrix products: 13.3 us -> 0 us
    ppermute x4 -> x8, waiting for transfers between devices: 82.4 us -> 40.4 us  [shifted(): return lax.ppermute(block, axis, route)]
    psum x1, waiting for transfers between devices: 156 us -> 129 us  [on_device(): probe_grad = lax.psum(update, ('row', 'col'))]
    ppermute x4 -> x8, starting transfers between devices: 49.9 us -> 26.5 us  [shifted(): return lax.ppermute(block, axis, route)]
    pallas_call x0 -> x1, Pallas kernels: none -> 21.7 us  [gradients(): pl.pallas_call(kernel, grid_spec=pltpu.PrefetchScalarGridSpec(num_scalar_...]
    another operation x9 -> x0, loops' own time: 13.6 us -> none  [the longest x8 8.14 us: visit(): return lax.cond(alive[number], work, lambda inner: inner, carried)]
    dynamic_update_slice x2 -> x0, local copies, waits for them, and re-layouts: 13.5 us -> none  [add_patch(): lax.dynamic_update_slice(totals, previous + term, (zero_index, start_row,...]
    dot_general x32 -> x0, matrix products: 13.3 us -> none  [the longest x16 6.66 us: left_dot(): jnp.einsum('ab,kbc->kac', table, matrix, preferred_element_type=jnp.float32)]
    ppermute x4 -> x0, starting transfers between devices: 9.47 us -> none  [the longest x2 6.9 us: extended_2(): lax.ppermute(lax.slice_in_dim(block, block.shape[dim] - width, None, axis...]
  transfers between devices with their start and end apart: 9 -> 9, of which waited for: 7 -> 8; matrix products, arithmetic and copies ran while one was open for 4% -> 3% of each run, Pallas kernels for 0% -> 0%
where the time goes in v1:
time: 250 us
  waiting for transfers between devices  169 us (68%)
  starting transfers between devices  26.6 us (11%)
  Pallas kernels  21.7 us (9%)
  between operations  14.8 us (6%)
  other arithmetic  8.69 us (3%)
  local copies, waits for them, and re-layouts  8.61 us (3%)
    psum x1, waiting for transfers between devices, on_device(): probe_grad = lax.psum(update, ('row', 'col'))  129 us
    ppermute x8, waiting for transfers between devices, shifted(): return lax.ppermute(block, axis, route)  40.4 us
    ppermute x8, starting transfers between devices, shifted(): return lax.ppermute(block, axis, route)  26.5 us
    pallas_call x1, Pallas kernels, gradients(): pl.pallas_call(kernel, grid_spec=pltpu.PrefetchScalarGridSpec(num_scalar_...  21.7 us
  transfers between devices with their start and end apart: 9, of which 8 were waited for; matrix products, arithmetic and copies ran while one was open for 3% of the time, Pallas kernels for 0%

profile of v1, /device:TPU:0, one launch (start us, length us, event | category | flops | bytes accessed | tf_op | source)
XLA Modules:
  0.0 249.5 jit_solution(4586911753808305947)
XLA Ops:
  7.2 0.0 copy-start.1
  7.2 0.0 all-reduce.2.cloned.1.call-start
  7.2 1.4 fusion.5
  8.6 1.3 collective-permute-start.1
  9.9 5.6 %collective-permute-start = (f32[2,512,128]{2,1,0:T(8,128)S(1)}, f32[2,512,128]{2,1,0:T(8,128)S(1)}, u32[]{:S(2)}, u32[]{:S(2)}) collective-permute-start(f32[2,512,128]{2,1,0:T(8,128)S(1)} %get-tuple-element.63), channel_id=1, source_target_pairs={{0,1},{1,2},{2,3},{4,5},{5,6},{6,7},{8,9},{9,10},{10,11},{12,13},{... | collective-permute-start | bytes 1572872 | tf_op jit(solution)/shard_map/ppermute | solution.py:19
  15.5 0.0 copy-done.1
  15.5 0.1 fusion.4
  15.6 0.0 copy-start.4
  15.6 9.8 %collective-permute-done.1.right_ref = f32[2,512,128]{2,1,0:T(8,128)S(1)} collective-permute-done((f32[2,512,128]{2,1,0:T(8,128)S(1)}, f32[2,512,128]{2,1,0:T(8,128)S(1)}, u32[]{:S(2)}, u32[]{:S(2)}) %collective-permute-start.1) | collective-permute-done | bytes 524320 | tf_op jit(solution)/shard_map/ppermute | solution.py:19
  25.5 0.0 copy-start.2
  25.5 1.2 collective-permute-done.left_ref
  26.7 0.0 copy-start.3
  26.7 0.1 pad_maximum_fusion
  26.8 2.2 collective-permute-start.2
  29.0 0.1 pad_maximum_fusion.1
  29.0 0.0 copy-done.2
  29.0 1.3 collective-permute-start.3
  31.0 0.0 copy-done.4
  31.0 0.6 subtract_bitcast_fusion
  31.6 0.0 collective-permute-done.2.top_ref
  31.6 2.8 %collective-permute-done.3.bottom_ref = f32[2,128,768]{2,1,0:T(8,128)} collective-permute-done((f32[2,128,768]{2,1,0:T(8,128)S(1)}, f32[2,128,768]{2,1,0:T(8,128)}, u32[]{:S(2)}, u32[]{:S(2)}) %collective-permute-start.3) | collective-permute-done | bytes 786464 | tf_op jit(solution)/shard_map/ppermute | solution.py:19
  34.3 0.0 copy-done.3
  34.3 21.7 %shard_map.77 = (f32[2,128,768]{2,1,0:T(8,128)}, f32[2,512,768]{2,1,0:T(8,128)}, f32[2,128,768]{2,1,0:T(8,128)}, f32[2,4,256,256]{3,2,1,0:T(8,128)}) custom-call(s32[8]{0:T(128)} %get-tuple-element.69.rows_ref, s32[8]{0:T(128)} %get-tuple-element.68.cols_ref, s32[1]{0:T(128)} %bitcast.5.count_ref, f32[2,512,512]{2,1,0:T(8,128)} %object_ref.1, ...), custom_call_target="tpu_custom_call" | custom-call | flops 8589934592 | bytes 16777216 | tf_op jit(solution)/shard_map/pallas_call | solution.py:257
  56.0 10.5 %collective-permute-start.4 = (f32[2,128,768]{2,1,0:T(8,128)}, f32[2,128,768]{2,1,0:T(8,128)S(1)}, u32[]{:S(2)}, u32[]{:S(2)}) collective-permute-start(f32[2,128,768]{2,1,0:T(8,128)} %get-tuple-element.55), channel_id=1, source_target_pairs={{0,4},{4,8},{8,12},{12,16},{16,20},{20,24},{24,28},{1,5},{5,9},{9,... | collective-permute-start | bytes 2359304 | tf_op jit(solution)/shard_map/ppermute | solution.py:19
  66.5 1.3 collective-permute-start.5
  67.8 0.8 collective-permute-done.4
  68.6 2.1 add_dynamic-update-slice_fusion
  70.7 19.4 %collective-permute-done.5 = f32[2,128,768]{2,1,0:T(8,128)S(1)} collective-permute-done((f32[2,128,768]{2,1,0:T(8,128)}, f32[2,128,768]{2,1,0:T(8,128)S(1)}, u32[]{:S(2)}, u32[]{:S(2)}) %collective-permute-start.5) | collective-permute-done | bytes 786464 | tf_op jit(solution)/shard_map/ppermute | solution.py:19
  90.0 2.1 fusion
  92.2 0.0 copy-start
  92.2 2.4 fusion.3
  94.6 3.1 %collective-permute-start.6 = (f32[2,512,128]{2,1,0:T(8,128)}, f32[2,512,128]{2,1,0:T(8,128)}, u32[]{:S(2)}, u32[]{:S(2)}) collective-permute-start(f32[2,512,128]{2,1,0:T(8,128)} %get-tuple-element.59), channel_id=1, source_target_pairs={{0,1},{1,2},{2,3},{4,5},{5,6},{6,7},{8,9},{9,10},{10,11},{12,13},{... | collective-permute-start | bytes 1572872 | tf_op jit(solution)/shard_map/ppermute | solution.py:19
  97.7 0.0 all-reduce.2.cloned.1.call-update
  97.7 1.3 collective-permute-start.7
  99.0 0.0 copy-done
  99.0 1.6 slice.158
  100.6 3.3 %collective-permute-done.6 = f32[2,512,128]{2,1,0:T(8,128)} collective-permute-done((f32[2,512,128]{2,1,0:T(8,128)}, f32[2,512,128]{2,1,0:T(8,128)}, u32[]{:S(2)}, u32[]{:S(2)}) %collective-permute-start.6) | collective-permute-done | bytes 524320 | tf_op jit(solution)/shard_map/ppermute | solution.py:19
  103.9 1.9 fusion.2
  105.8 3.2 %collective-permute-done.7 = f32[2,512,128]{2,1,0:T(8,128)S(1)} collective-permute-done((f32[2,512,128]{2,1,0:T(8,128)}, f32[2,512,128]{2,1,0:T(8,128)S(1)}, u32[]{:S(2)}, u32[]{:S(2)}) %collective-permute-start.7) | collective-permute-done | bytes 524320 | tf_op jit(solution)/shard_map/ppermute | solution.py:19
  109.0 1.9 fusion.1
  110.9 128.7 %all-reduce.2.cloned.1.call-done = f32[2,4,256,256]{3,2,1,0:T(8,128)} async-done(((f32[2,4,256,256]{3,2,1,0:T(8,128)}), f32[2,4,256,256]{3,2,1,0:T(8,128)}) %all-reduce.2.cloned.1.call-update) | async-done | bytes 2097168 | tf_op jit(solution)/shard_map/psum | solution.py:314
  239.6 3.0 %copy.14 = f32[2,4,256,256]{3,2,1,0:T(8,128)} copy(f32[2,4,256,256]{3,2,1,0:T(8,128)} %all-reduce.2.cloned.1.call-done) | data formatting | bytes 4194304
  (2 shorter events, 0.0 us)
Async XLA Ops:
  7.2 8.4 %copy-start.1 = (f32[2,512,512]{2,1,0:T(8,128)S(1)}, f32[2,512,512]{2,1,0:T(8,128)}, u32[]{:S(2)}) copy-start(f32[2,512,512]{2,1,0:T(8,128)} %object_ref.1) | copy-start | bytes 6291460
  7.2 232.5 %all-reduce.2.cloned.1.call-start = ((), (), s32[]{:S(2)}) async-start(), calls=%async_computation | async-start | bytes 4194304 | tf_op jit(solution)/shard_map/psum | solution.py:314
  8.6 16.8 %collective-permute-start.1 = (f32[2,512,128]{2,1,0:T(8,128)S(1)}, f32[2,512,128]{2,1,0:T(8,128)S(1)}, u32[]{:S(2)}, u32[]{:S(2)}) collective-permute-start(f32[2,512,128]{2,1,0:T(8,128)S(1)} %get-tuple-element.62), channel_id=1, source_target_pairs={{1,0},{2,1},{3,2},{5,4},{6,5},{7,6},{9,8},{10,9},{11,10},{13,12},{... | collective-permute-start | bytes 1572872 | tf_op jit(solution)/shard_map/ppermute | solution.py:19
  9.9 16.7 %collective-permute-start = (f32[2,512,128]{2,1,0:T(8,128)S(1)}, f32[2,512,128]{2,1,0:T(8,128)S(1)}, u32[]{:S(2)}, u32[]{:S(2)}) collective-permute-start(f32[2,512,128]{2,1,0:T(8,128)S(1)} %get-tuple-element.63), channel_id=1, source_target_pairs={{0,1},{1,2},{2,3},{4,5},{5,6},{6,7},{8,9},{9,10},{10,11},{12,13},{... | collective-permute-start | bytes 1572872 | tf_op jit(solution)/shard_map/ppermute | solution.py:19
  15.6 15.3 %copy-start.4 = (s32[2,8]{1,0:T(2,128)S(1)}, s32[2,8]{1,0:T(2,128)}, u32[]{:S(2)}) copy-start(s32[2,8]{1,0:T(2,128)} %param.17) | copy-start | bytes 196
  25.5 3.5 %copy-start.2 = (f32[2,512,128]{2,1,0:T(8,128)}, f32[2,512,128]{2,1,0:T(8,128)S(1)}, u32[]{:S(2)}) copy-start(f32[2,512,128]{2,1,0:T(8,128)S(1)} %collective-permute-done.1.right_ref) | copy-start | bytes 1572868
  26.7 7.7 %copy-start.3 = (f32[2,512,128]{2,1,0:T(8,128)}, f32[2,512,128]{2,1,0:T(8,128)S(1)}, u32[]{:S(2)}) copy-start(f32[2,512,128]{2,1,0:T(8,128)S(1)} %collective-permute-done.left_ref) | copy-start | bytes 1572868
  26.8 4.8 %collective-permute-start.2 = (f32[2,128,768]{2,1,0:T(8,128)S(1)}, f32[2,128,768]{2,1,0:T(8,128)}, u32[]{:S(2)}, u32[]{:S(2)}) collective-permute-start(f32[2,128,768]{2,1,0:T(8,128)S(1)} %pad_maximum_fusion), channel_id=1, source_target_pairs={{0,4},{4,8},{8,12},{12,16},{16,20},{20,24},{24,28},{1,5},{5,9},{9,... | collective-permute-start | bytes 2359304 | tf_op jit(solution)/shard_map/ppermute | solution.py:19
  29.0 5.3 %collective-permute-start.3 = (f32[2,128,768]{2,1,0:T(8,128)S(1)}, f32[2,128,768]{2,1,0:T(8,128)}, u32[]{:S(2)}, u32[]{:S(2)}) collective-permute-start(f32[2,128,768]{2,1,0:T(8,128)S(1)} %pad_maximum_fusion.1), channel_id=1, source_target_pairs={{4,0},{8,4},{12,8},{16,12},{20,16},{24,20},{28,24},{5,1},{9,5},{13... | collective-permute-start | bytes 2359304 | tf_op jit(solution)/shard_map/ppermute | solution.py:19
  56.0 12.5 %collective-permute-start.4 = (f32[2,128,768]{2,1,0:T(8,128)}, f32[2,128,768]{2,1,0:T(8,128)S(1)}, u32[]{:S(2)}, u32[]{:S(2)}) collective-permute-start(f32[2,128,768]{2,1,0:T(8,128)} %get-tuple-element.55), channel_id=1, source_target_pairs={{0,4},{4,8},{8,12},{12,16},{16,20},{20,24},{24,28},{1,5},{5,9},{9,... | collective-permute-start | bytes 2359304 | tf_op jit(solution)/shard_map/ppermute | solution.py:19
  66.5 23.5 %collective-permute-start.5 = (f32[2,128,768]{2,1,0:T(8,128)}, f32[2,128,768]{2,1,0:T(8,128)S(1)}, u32[]{:S(2)}, u32[]{:S(2)}) collective-permute-start(f32[2,128,768]{2,1,0:T(8,128)} %get-tuple-element.56), channel_id=1, source_target_pairs={{4,0},{8,4},{12,8},{16,12},{20,16},{24,20},{28,24},{5,1},{9,5},{13... | collective-permute-start | bytes 2359304 | tf_op jit(solution)/shard_map/ppermute | solution.py:19
  92.2 6.9 %copy-start = (f32[2,512,768]{2,1,0:T(8,128)S(1)}, f32[2,512,768]{2,1,0:T(8,128)}, u32[]{:S(2)}) copy-start(f32[2,512,768]{2,1,0:T(8,128)} %fusion) | copy-start | bytes 9437188
  94.6 9.3 %collective-permute-start.6 = (f32[2,512,128]{2,1,0:T(8,128)}, f32[2,512,128]{2,1,0:T(8,128)}, u32[]{:S(2)}, u32[]{:S(2)}) collective-permute-start(f32[2,512,128]{2,1,0:T(8,128)} %get-tuple-element.59), channel_id=1, source_target_pairs={{0,1},{1,2},{2,3},{4,5},{5,6},{6,7},{8,9},{9,10},{10,11},{12,13},{... | collective-permute-start | bytes 1572872 | tf_op jit(solution)/shard_map/ppermute | solution.py:19
  97.7 11.3 %collective-permute-start.7 = (f32[2,512,128]{2,1,0:T(8,128)}, f32[2,512,128]{2,1,0:T(8,128)S(1)}, u32[]{:S(2)}, u32[]{:S(2)}) collective-permute-start(f32[2,512,128]{2,1,0:T(8,128)} %get-tuple-element.58), channel_id=1, source_target_pairs={{1,0},{2,1},{3,2},{5,4},{6,5},{7,6},{9,8},{10,9},{11,10},{13,12},{... | collective-permute-start | bytes 1572872 | tf_op jit(solution)/shard_map/ppermute | solution.py:19
Sparse Core Ops, SparseCore 0:
  97.8 141.7 all-reduce.1

commit v2 on v1

--- a/solution.py
+++ b/solution.py
@@ -11,12 +11,6 @@
 
 F32 = jnp.float32
 BF16 = jnp.bfloat16
-
-
-def shifted(block, axis, distance):
-    devices = range(lax.axis_size(axis))
-    route = [(i - distance, i) for i in devices if i - distance in devices]
-    return lax.ppermute(block, axis, route)
 
 
 def tables(length):
@@ -290,6 +284,364 @@
     )(rows, cols, count, object_field, left, right, top, bottom, probe, patterns, patterns, table)
 
 
+class Move:
+    def __init__(self, src, dst, sems, index, target, sends=None, lands=None):
+        self.copy = pltpu.make_async_remote_copy(
+            src_ref=src,
+            dst_ref=dst,
+            send_sem=sems[0].at[index],
+            recv_sem=sems[1].at[index],
+            device_id=target,
+            device_id_type=pl.DeviceIdType.MESH,
+        )
+        self.sends = sends
+        self.lands = lands
+
+    def start(self):
+        when(self.sends, self.copy.start)
+
+    def arrive(self):
+        when(self.lands, self.copy.wait_recv)
+
+    def leave(self):
+        when(self.sends, self.copy.wait_send)
+
+
+def when(condition, action):
+    if condition is None:
+        action()
+    else:
+        pl.when(condition)(lambda: action())
+
+
+class Place:
+    def __init__(self):
+        self.row, self.col = lax.axis_index("row"), lax.axis_index("col")
+        self.rows, self.cols = lax.axis_size("row"), lax.axis_size("col")
+        self.has_up, self.has_down = self.row > 0, self.row < self.rows - 1
+        self.has_left, self.has_right = self.col > 0, self.col < self.cols - 1
+        self.up, self.down = (self.row - 1, self.col), (self.row + 1, self.col)
+        self.left, self.right = (self.row, self.col - 1), (self.row, self.col + 1)
+
+    def greet(self, others=()):
+        barrier = pltpu.get_barrier_semaphore()
+        near = [
+            (self.has_up, self.up),
+            (self.has_down, self.down),
+            (self.has_left, self.left),
+            (self.has_right, self.right),
+        ]
+
+        def signal(target):
+            pl.semaphore_signal(
+                barrier, inc=1, device_id=target, device_id_type=pl.DeviceIdType.MESH
+            )
+
+        for condition, target in near:
+            when(condition, lambda target=target: signal(target))
+        for target in others:
+            signal(target)
+        peers = sum(condition.astype(jnp.int32) for condition, _ in near)
+        pl.semaphore_wait(barrier, peers + len(others))
+
+
+def halo_kernel(object_ref, left_ref, right_ref, top_ref, bottom_ref, send_sems, recv_sems):
+    me = Place()
+    tile_rows, tile_cols = object_ref.shape[1:]
+    margin = top_ref.shape[1]
+    sems = (send_sems, recv_sems)
+    head, tail = pl.ds(0, margin), pl.ds(tile_rows - margin, margin)
+    bands = [head, tail]
+    if tile_rows > 2 * margin:
+        bands.append(pl.ds(margin, tile_rows - 2 * margin))
+    first, final = pl.ds(0, margin), pl.ds(tile_cols - margin, margin)
+    centre = pl.ds(margin, tile_cols)
+    beyond = pl.ds(margin + tile_cols, margin)
+    me.greet()
+    count = iter(range(send_sems.shape[0]))
+
+    sides = []
+    for band in bands:
+        sides.append(
+            (
+                Move(object_ref.at[:, band, final], left_ref.at[:, band, :], sems, next(count),
+                     me.right, me.has_right, me.has_left),
+                Move(object_ref.at[:, band, first], right_ref.at[:, band, :], sems, next(count),
+                     me.left, me.has_left, me.has_right),
+            )
+        )
+    below = Move(object_ref.at[:, tail, :], top_ref.at[:, :, centre], sems, next(count),
+                 me.down, me.has_down, me.has_up)
+    above = Move(object_ref.at[:, head, :], bottom_ref.at[:, :, centre], sems, next(count),
+                 me.up, me.has_up, me.has_down)
+    moves = [move for pair in sides for move in pair] + [below, above]
+    for move in moves:
+        move.start()
+    corners = []
+    for number, (band, target, sends, lands, out_ref) in enumerate(
+        [
+            (head, me.up, me.has_up, me.has_down, bottom_ref),
+            (tail, me.down, me.has_down, me.has_up, top_ref),
+        ]
+    ):
+        for side, (src_ref, there, has) in enumerate(
+            [(left_ref, first, me.has_left), (right_ref, beyond, me.has_right)]
+        ):
+            sides[number][side].arrive()
+            move = Move(src_ref.at[:, band, :], out_ref.at[:, :, there], sems, next(count),
+                        target, jnp.logical_and(sends, has), jnp.logical_and(lands, has))
+            move.start()
+            corners.append(move)
+    for pair in sides[2:]:
+        for move in pair:
+            move.arrive()
+    for move in [below, above] + corners:
+        move.arrive()
+    for move in moves + corners:
+        move.leave()
+
+
+def halo(object_field, margin):
+    tile_rows, tile_cols = object_field.shape[1:]
+    side = jax.ShapeDtypeStruct((2, tile_rows, margin), F32)
+    edge = jax.ShapeDtypeStruct((2, margin, tile_cols + 2 * margin), F32)
+    return pl.pallas_call(
+        halo_kernel,
+        in_specs=[pl.BlockSpec(memory_space=pl.ANY)],
+        out_specs=[pl.BlockSpec(memory_space=pl.ANY)] * 4,
+        out_shape=[side, side, edge, edge],
+        scratch_shapes=[pltpu.SemaphoreType.DMA((12,)), pltpu.SemaphoreType.DMA((12,))],
+        compiler_params=pltpu.CompilerParams(collective_id=0, has_side_effects=True),
+    )(object_field)
+
+
+def bits_of(count):
+    return [1 << i for i in range(count.bit_length() - 1)]
+
+
+def last_kernel(
+    up_ref, middle_ref, down_ref, update_ref,
+    object_ref, probe_ref,
+    above, below, from_left, from_right, edges, total, landed,
+    send_sems, recv_sems, sum_send, sum_recv, local_sems,
+):
+    me = Place()
+    tile_rows, tile_cols = object_ref.shape[1:]
+    margin = up_ref.shape[1]
+    sems = (send_sems, recv_sems)
+    head, tail = pl.ds(0, margin), pl.ds(tile_rows - margin, margin)
+    first, beyond = pl.ds(0, margin), pl.ds(margin + tile_cols, margin)
+    centre = pl.ds(margin, tile_cols)
+
+    row_bits = [("row", bit) for bit in bits_of(me.rows)]
+    col_bits = [("col", bit) for bit in bits_of(me.cols)]
+    orders = [row_bits + col_bits, row_bits[:1] + row_bits[:0:-1] + col_bits]
+
+    def partner(axis, bit):
+        flip = lambda at: at + bit - 2 * bit * (at // bit % 2)
+        return (flip(me.row), me.col) if axis == "row" else (me.row, flip(me.col))
+
+    def half_of(axis, bit):
+        return (me.row if axis == "row" else me.col) // bit % 2
+
+    local = [
+        pltpu.make_async_copy(update_ref, total, local_sems.at[0]),
+        pltpu.make_async_copy(middle_ref.at[:, :, centre], object_ref, local_sems.at[1]),
+    ]
+    for side, cols in enumerate((first, beyond)):
+        for end, band in enumerate((head, tail)):
+            local.append(
+                pltpu.make_async_copy(
+                    middle_ref.at[:, band, cols],
+                    edges.at[side, end],
+                    local_sems.at[2 + 2 * side + end],
+                )
+            )
+    for copy in local:
+        copy.start()
+    me.greet([partner(axis, bit) for axis, bit in orders[0] if bit > 1])
+
+    count = iter(range(send_sems.shape[0]))
+    corners = []
+    for cols in (first, beyond):
+        corners.append(
+            (
+                Move(down_ref.at[:, :, cols], above.at[:, :, cols], sems, next(count),
+                     me.down, me.has_down, me.has_up),
+                Move(up_ref.at[:, :, cols], below.at[:, :, cols], sems, next(count),
+                     me.up, me.has_up, me.has_down),
+            )
+        )
+    for pair in corners:
+        for move in pair:
+            move.start()
+
+    size = update_ref.shape[0]
+    bases = [[0], [0]]
+
+    def halving(stream, step):
+        lanes = pl.ds(stream * LANES, LANES)
+        axis, bit = orders[stream][step]
+        rows = size >> (step + 1)
+        half = half_of(axis, bit)
+        base = bases[stream][step]
+        keep = pl.multiple_of(base + half * rows, SUB)
+        give = pl.multiple_of(base + (1 - half) * rows, SUB)
+        bases[stream].append(keep)
+        source = update_ref if step == 0 else total
+        return Move(
+            source.at[pl.ds(give, rows), lanes],
+            landed.at[pl.ds(size - 2 * rows, rows), lanes],
+            (sum_send.at[stream], sum_recv.at[stream]), step, partner(axis, bit),
+        )
+
+    def add_half(stream, step, out_ref):
+        lanes = pl.ds(stream * LANES, LANES)
+        rows = size >> (step + 1)
+        here = (pl.ds(bases[stream][step + 1], rows), lanes)
+        out_ref[here] = total[here] + landed[pl.ds(size - 2 * rows, rows), lanes]
+
+    def doubling(stream, step):
+        lanes = pl.ds(stream * LANES, LANES)
+        axis, bit = orders[stream][step]
+        here = (pl.ds(bases[stream][step + 1], size >> (step + 1)), lanes)
+        return Move(
+            probe_ref.at[here], probe_ref.at[here],
+            (sum_send.at[stream], sum_recv.at[stream]), steps + step, partner(axis, bit),
+        )
+
+    steps = len(orders[0])
+    streams = range(2)
+    sums = []
+    current = [halving(stream, 0) for stream in streams]
+    for move in current:
+        move.start()
+
+    flats = []
+    if tile_rows > 2 * margin:
+        inner = pl.ds(margin, tile_rows - 2 * margin)
+        flats = [
+            Move(middle_ref.at[:, inner, beyond], from_left.at[:, inner, :], sems, next(count),
+                 me.right, me.has_right, me.has_left),
+            Move(middle_ref.at[:, inner, first], from_right.at[:, inner, :], sems, next(count),
+                 me.left, me.has_left, me.has_right),
+        ]
+    flats += [
+        Move(down_ref.at[:, :, centre], above.at[:, :, centre], sems, next(count),
+             me.down, me.has_down, me.has_up),
+        Move(up_ref.at[:, :, centre], below.at[:, :, centre], sems, next(count),
+             me.up, me.has_up, me.has_down),
+    ]
+    for move in flats:
+        move.start()
+    for copy in local:
+        copy.wait()
+
+    ends = []
+
+    def send_ends():
+        for side, (cols, out_ref, target, sends, lands) in enumerate(
+            [
+                (first, from_right, me.left, me.has_left, me.has_right),
+                (beyond, from_left, me.right, me.has_right, me.has_left),
+            ]
+        ):
+            for end, (band, got, has) in enumerate(
+                [(head, above, me.has_up), (tail, below, me.has_down)]
+            ):
+                corners[side][end].arrive()
+
+                def add(side=side, end=end, got=got, cols=cols):
+                    edges[side, end] += got[:, :, cols]
+
+                when(has, add)
+                move = Move(edges.at[side, end], out_ref.at[:, band, :], sems, next(count),
+                            target, sends, lands)
+                move.start()
+                ends.append(move)
+
+    for step in range(steps):
+        for stream in streams:
+            move = current[stream]
+            move.arrive()
+            sums.append(move)
+            add_half(stream, step, total if step < steps - 1 else probe_ref)
+            if step < steps - 1:
+                current[stream] = halving(stream, step + 1)
+            else:
+                current[stream] = doubling(stream, step)
+            current[stream].start()
+        if step == 0:
+            send_ends()
+    for step in range(steps - 1, -1, -1):
+        for stream in streams:
+            move = current[stream]
+            move.arrive()
+            sums.append(move)
+            if step > 0:
+                current[stream] = doubling(stream, step - 1)
+                current[stream].start()
+
+    for move in flats + ends:
+        move.arrive()
+
+    def from_above():
+        object_ref[:, :margin, :] += above[:, :, margin : margin + tile_cols]
+
+    def from_below():
+        object_ref[:, tile_rows - margin :, :] += below[:, :, margin : margin + tile_cols]
+
+    def add_left():
+        object_ref[:, :, :margin] += from_left[...]
+
+    def add_right():
+        object_ref[:, :, tile_cols - margin :] += from_right[...]
+
+    when(me.has_up, from_above)
+    when(me.has_down, from_below)
+    when(me.has_left, add_left)
+    when(me.has_right, add_right)
+    for move in [move for pair in corners for move in pair] + flats + ends + sums:
+        move.leave()
+
+
+def finish(up, middle, down, update):
+    margin = up.shape[1]
+    tile_rows = middle.shape[1]
+    tile_cols = middle.shape[2] - 2 * margin
+    width = update.shape[-1]
+    flat = update.reshape(-1, width)
+    steps = len(bits_of(lax.axis_size("row") * lax.axis_size("col")))
+    vmem = pl.BlockSpec(memory_space=pltpu.VMEM)
+    object_grad, probe_grad = pl.pallas_call(
+        last_kernel,
+        in_specs=[pl.BlockSpec(memory_space=pl.ANY)] * 4,
+        out_specs=[vmem, vmem],
+        out_shape=[
+            jax.ShapeDtypeStruct((2, tile_rows, tile_cols), F32),
+            jax.ShapeDtypeStruct(flat.shape, F32),
+        ],
+        scratch_shapes=[
+            pltpu.VMEM(up.shape, F32),
+            pltpu.VMEM(up.shape, F32),
+            pltpu.VMEM((2, tile_rows, margin), F32),
+            pltpu.VMEM((2, tile_rows, margin), F32),
+            pltpu.VMEM((2, 2, 2, margin, margin), F32),
+            pltpu.VMEM(flat.shape, F32),
+            pltpu.VMEM(flat.shape, F32),
+            pltpu.SemaphoreType.DMA((12,)),
+            pltpu.SemaphoreType.DMA((12,)),
+            pltpu.SemaphoreType.DMA((2, 2 * steps)),
+            pltpu.SemaphoreType.DMA((2, 2 * steps)),
+            pltpu.SemaphoreType.DMA((6,)),
+        ],
+        compiler_params=pltpu.CompilerParams(
+            collective_id=1, has_side_effects=True, vmem_limit_bytes=40 * 2**20
+        ),
+    )(up, middle, down, flat)
+    return object_grad, probe_grad.reshape(update.shape)
+
+
 def on_device(object_field, probe, patterns, offsets, counts):
     tile_rows, tile_cols = object_field.shape[1:]
     width = patterns.shape[1]
@@ -297,30 +649,12 @@
     base_row = lax.axis_index("row") * tile_rows - margin
     base_col = lax.axis_index("col") * tile_cols - margin
     table = jnp.asarray(tables(width))
-
-    left = shifted(object_field[:, :, tile_cols - margin :], "col", 1)
-    right = shifted(object_field[:, :, :margin], "col", -1)
-    tail = slice(tile_rows - margin, None)
-    head = slice(None, margin)
-    lower = jnp.concatenate([left[:, tail], object_field[:, tail], right[:, tail]], axis=2)
-    upper = jnp.concatenate([left[:, head], object_field[:, head], right[:, head]], axis=2)
-    top = shifted(lower, "row", 1)
-    bottom = shifted(upper, "row", -1)
-
+    left, right, top, bottom = halo(object_field, margin)
     up, middle, down, update = gradients(
         offsets[0] - base_row, offsets[1] - base_col, counts.reshape(-1),
         object_field, left, right, top, bottom, probe, patterns, table,
     )
-    probe_grad = lax.psum(update, ("row", "col"))
-    from_above = shifted(down, "row", 1)
-    from_below = shifted(up, "row", -1)
-    middle = middle.at[:, head].add(from_above).at[:, tail].add(from_below)
-    from_left = shifted(middle[:, :, tile_cols + margin :], "col", 1)
-    from_right = shifted(middle[:, :, :margin], "col", -1)
-    object_grad = middle[:, :, margin : margin + tile_cols]
-    object_grad = object_grad.at[:, :, :margin].add(from_left)
-    object_grad = object_grad.at[:, :, tile_cols - margin :].add(from_right)
-    return (object_grad, probe_grad)
+    return finish(up, middle, down, update)
 
 
 def solution(mesh):

time: 250 us -> 125 us (0.50)
  the two profiles are of different devices: /device:TPU:0 before, /device:TPU:11 now
where the time goes in v2:
time: 125 us; the launch traced here: 126 us
  Pallas kernels  115 us (92%)
  local copies, waits for them, and re-layouts  8.38 us (7%)
  other arithmetic  1.35 us (1%)
  between operations  1.32 us (1%)
    pallas_call x1, Pallas kernels, finish(): pl.pallas_call(last_kernel, in_specs=[pl.BlockSpec(memory_space=pl.ANY)]...  65.4 us
    pallas_call x1, Pallas kernels, gradients(): pl.pallas_call(kernel, grid_spec=pltpu.PrefetchScalarGridSpec(num_scalar_...  28.4 us
    pallas_call x1, Pallas kernels, halo(): pl.pallas_call(halo_kernel, in_specs=[pl.BlockSpec(memory_space=pl.ANY)],...  21.4 us
    unnamed x10, local copies, waits for them, and re-layouts  8.38 us

profile of v2, /device:TPU:11, one launch (start us, length us, event | category | flops | bytes accessed | tf_op | source)
XLA Modules:
  0.0 126.2 jit_solution(1577018085686104606)
XLA Ops:
  1.3 1.4 %subtract_bitcast_fusion = (s32[8]{0:T(128)}, s32[8]{0:T(128)}) fusion(s32[2,8]{1,0:T(2,128)} %param.9, s32[]{:T(128)S(6)} %sub.26, s32[]{:T(128)S(6)} %sub.22), kind=kLoop, calls=%fused_computation | loop fusion | flops 16 | bytes 136 | tf_op jit(solution)/shard_map/sub | solution.py:654
  2.6 21.4 %shard_map.77 = (f32[2,512,128]{2,1,0:T(8,128)}, f32[2,512,128]{2,1,0:T(8,128)}, f32[2,128,768]{2,1,0:T(8,128)}, f32[2,128,768]{2,1,0:T(8,128)}) custom-call(f32[2,512,512]{2,1,0:T(8,128)} %object_ref.3), custom_call_target="tpu_custom_call" | custom-call | tf_op jit(solution)/shard_map/pallas_call | solution.py:408
  24.0 28.4 %shard_map.78 = (f32[2,128,768]{2,1,0:T(8,128)}, f32[2,512,768]{2,1,0:T(8,128)}, f32[2,128,768]{2,1,0:T(8,128)}, f32[2,4,256,256]{3,2,1,0:T(8,128)}) custom-call(s32[8]{0:T(128)} %get-tuple-element.23.rows_ref, s32[8]{0:T(128)} %get-tuple-element.22.cols_ref, s32[1]{0:T(128)} %bitcast.7.count_ref, f32[2,512,512]{2,1,0:T(8,128)} %object_ref.3, ...), custom_call_target="tpu_custom_call" | custom-call | flops 8589934592 | bytes 16777216 | tf_op jit(solution)/shard_map/pallas_call | solution.py:251
  52.4 0.0 copy-start
  52.4 1.9 %copy-done = f32[2,512,768]{2,1,0:T(8,128)S(1)} copy-done((f32[2,512,768]{2,1,0:T(8,128)S(1)}, f32[2,512,768]{2,1,0:T(8,128)}, u32[]{:S(2)}) %copy-start) | copy-done | bytes 3145752
  54.3 0.0 copy-start.1
  54.3 1.6 %copy-done.1 = f32[2,4,256,256]{3,2,1,0:T(8,128)S(1)} copy-done((f32[2,4,256,256]{3,2,1,0:T(8,128)S(1)}, f32[2,4,256,256]{3,2,1,0:T(8,128)}, u32[]{:S(2)}) %copy-start.1) | copy-done | bytes 2097176
  55.9 0.0 copy-start.2
  55.9 1.1 copy-done.2
  57.0 0.0 copy-start.3
  57.0 1.1 copy-done.3
  58.1 65.4 %shard_map.79 = (f32[2,512,512]{2,1,0:T(8,128)S(1)}, f32[2048,256]{1,0:T(8,128)S(1)}) custom-call(f32[2,128,768]{2,1,0:T(8,128)S(1)} %copy-done.2, f32[2,512,768]{2,1,0:T(8,128)S(1)} %copy-done, f32[2,128,768]{2,1,0:T(8,128)S(1)} %copy-done.3, f32[2048,256]{1,0:T(8,128)S(1)} %bitcast.8), custom_call_target="tpu_custom_call" | custom-call | tf_op jit(solution)/shard_map/pallas_call | solution.py:616
  123.5 1.3 %copy.11 = f32[2,512,512]{2,1,0:T(8,128)} copy(f32[2,512,512]{2,1,0:T(8,128)S(1)} %get-tuple-element.26) | data formatting | bytes 4194304
  124.9 1.3 %copy.12 = f32[2,4,256,256]{3,2,1,0:T(8,128)} copy(f32[2,4,256,256]{3,2,1,0:T(8,128)S(1)} %bitcast.9) | data formatting | bytes 4194304
Async XLA Ops:
  52.4 1.9 %copy-start = (f32[2,512,768]{2,1,0:T(8,128)S(1)}, f32[2,512,768]{2,1,0:T(8,128)}, u32[]{:S(2)}) copy-start(f32[2,512,768]{2,1,0:T(8,128)} %get-tuple-element.17.middle_ref) | copy-start | bytes 9437188
  54.3 1.6 %copy-start.1 = (f32[2,4,256,256]{3,2,1,0:T(8,128)S(1)}, f32[2,4,256,256]{3,2,1,0:T(8,128)}, u32[]{:S(2)}) copy-start(f32[2,4,256,256]{3,2,1,0:T(8,128)} %get-tuple-element.19) | copy-start | bytes 6291460
  55.9 1.1 copy-start.2
  57.0 1.1 copy-start.3

commit v3 on v2

--- a/solution.py
+++ b/solution.py
@@ -58,50 +58,72 @@
 
 
 def kernel(
-    rows_ref, cols_ref, count_ref,
-    object_ref, left_ref, right_ref, top_ref, bottom_ref, probe_ref, pattern_lo, pattern_hi, table_ref,
-    up_ref, middle_ref, down_ref, update_ref,
-    ext, totals, patch, field, residual, term, sems,
+    offsets_ref, count_ref,
+    extended_ref, probe_hbm, patterns_ref, table_hbm,
+    up_ref, middle_ref, down_ref, update_out,
+    window, pattern, probe_ref, table_ref, totals, update_ref, patch, mixed, field, residual,
+    measured_ref, term, sems,
 ):
-    number = pl.program_id(0)
-    last = pl.num_programs(0) - 1
-    tile_rows, tile_cols = object_ref.shape[1:]
-    margin = top_ref.shape[1]
+    margin, tile_rows = up_ref.shape[1], middle_ref.shape[1]
     modes, width = probe_ref.shape[1:3]
+    tile_cols = middle_ref.shape[2] - 2 * margin
     half = width // 2
     lanes = LANES
-
-    @pl.when(number == 0)
-    def _():
-        body = pl.ds(margin, tile_rows)
-        copies = [
-            pltpu.make_async_copy(object_ref, ext.at[:, body, pl.ds(margin, tile_cols)], sems.at[0]),
-            pltpu.make_async_copy(left_ref, ext.at[:, body, pl.ds(0, margin)], sems.at[1]),
+    tall, wide = window.shape[2:]
+    chunk = 16
+    live = count_ref[0, 0]
+    first_row = lax.axis_index("row") * tile_rows - margin
+    first_col = lax.axis_index("col") * tile_cols - margin
+
+    def corner(number):
+        row = offsets_ref[0, number] - first_row
+        col = offsets_ref[1, number] - first_col
+        row_base = jnp.minimum(row // SUB * SUB, totals.shape[1] - tall)
+        col_base = jnp.minimum(col // lanes * lanes, totals.shape[2] - wide)
+        return (
+            pl.multiple_of(row_base, SUB), row - row_base,
+            pl.multiple_of(col_base, lanes), col - col_base,
+        )
+
+    def fetches(number):
+        slot = lax.rem(number, 2)
+        row_base, _, col_base, _ = corner(number)
+        return [
             pltpu.make_async_copy(
-                right_ref, ext.at[:, body, pl.ds(margin + tile_cols, margin)], sems.at[2]
-            ),
-            pltpu.make_async_copy(top_ref, ext.at[:, pl.ds(0, margin), :], sems.at[3]),
+                extended_ref.at[:, pl.ds(row_base, tall), pl.ds(col_base, wide)],
+                window.at[slot], sems.at[slot, 0],
+            )
+        ] + [
             pltpu.make_async_copy(
-                bottom_ref, ext.at[:, pl.ds(margin + tile_rows, margin), :], sems.at[4]
-            ),
+                patterns_ref.at[number, :, pl.ds(side * half, half)],
+                pattern.at[slot, side], sems.at[slot, 1 + side],
+            )
+            for side in range(2)
         ]
-        for copy in copies:
-            copy.start()
-        totals[...] = jnp.zeros_like(totals)
-        update_ref[...] = jnp.zeros_like(update_ref)
-        for copy in copies:
+
+    constants = [
+        pltpu.make_async_copy(table_hbm, table_ref, sems.at[2, 0]),
+        pltpu.make_async_copy(probe_hbm, probe_ref, sems.at[2, 1]),
+    ]
+    for copy in fetches(0) + constants:
+        copy.start()
+    totals[...] = jnp.zeros_like(totals)
+    update_ref[...] = jnp.zeros_like(update_ref)
+    for copy in constants:
+        copy.wait()
+
+    def visit(number, carried):
+        slot = lax.rem(number, 2)
+        row_base, row_shift, base, shift = corner(number)
+
+        @pl.when(number + 1 < live)
+        def _():
+            for copy in fetches(number + 1):
+                copy.start()
+
+        for copy in fetches(number):
             copy.wait()
 
-    @pl.when(number < count_ref[0])
-    def _():
-        row = rows_ref[number]
-        col = cols_ref[number]
-        limit = ext.shape[2] - width - lanes
-        base = pl.multiple_of(jnp.minimum(col // lanes * lanes, limit), lanes)
-        shift = col - base
-        tall = width + SUB
-        row_base = pl.multiple_of(jnp.minimum(row // SUB * SUB, ext.shape[1] - tall), SUB)
-        row_shift = row - row_base
         lane = lax.broadcasted_iota(jnp.int32, (width, lanes), 1)
         back = lax.rem(lanes - shift, lanes)
         ahead = lax.rem(shift, lanes)
@@ -109,11 +131,7 @@
         for part in range(2):
             pieces = [
                 pltpu.roll(
-                    rows_up(
-                        ext[part, pl.ds(row_base, tall), pl.ds(base + t * lanes, lanes)], row_shift
-                    ),
-                    back,
-                    1,
+                    rows_up(window[slot, part, :, t * lanes : (t + 1) * lanes], row_shift), back, 1
                 )
                 for t in range(width // lanes + 1)
             ]
@@ -126,21 +144,29 @@
         l_even, l_odd = table_ref[2], table_ref[3]
         spread = table_ref[4]
 
-        intensity = [jnp.zeros((half, width), F32) for _ in range(2)]
+        for parity in range(2):
+            rows_of = pl.ds(parity, half, 2)
+            measured = jnp.concatenate(
+                [pattern[slot, 0, rows_of, :], pattern[slot, 1, rows_of, :]], axis=1
+            )
+            coarse = measured.astype(BF16)
+            fine = (measured - coarse.astype(F32)).astype(BF16)
+            measured_ref[parity] = mm(coarse, spread) + mm(fine, spread)
+
         for k in range(modes):
-            o_re, o_im = patch[0], patch[1]
-            p_re = probe_ref[0, k].astype(F32)
-            p_im = probe_ref[1, k].astype(F32)
-            x_re = p_re * o_re - p_im * o_im
-            x_im = p_re * o_im + p_im * o_re
-            s = jnp.concatenate(
-                [x_re[:, :half] + x_re[:, half:], x_im[:, :half] + x_im[:, half:]], axis=1
-            ).astype(BF16)
-            d = jnp.concatenate(
-                [x_re[:, :half] - x_re[:, half:], x_im[:, :half] - x_im[:, half:]], axis=1
-            ).astype(BF16)
-            y_even = mm(s, r_even)
-            y_odd = mm(d, r_odd)
+            for start in range(0, width, chunk):
+                here = slice(start, start + chunk)
+                o_re, o_im = patch[0, here], patch[1, here]
+                p_re = probe_ref[0, k, here].astype(F32)
+                p_im = probe_ref[1, k, here].astype(F32)
+                x_re = p_re * o_re - p_im * o_im
+                x_im = p_re * o_im + p_im * o_re
+                mixed[k, 0, here, :half] = (x_re[:, :half] + x_re[:, half:]).astype(BF16)
+                mixed[k, 0, here, half:] = (x_im[:, :half] + x_im[:, half:]).astype(BF16)
+                mixed[k, 1, here, :half] = (x_re[:, :half] - x_re[:, half:]).astype(BF16)
+                mixed[k, 1, here, half:] = (x_im[:, :half] - x_im[:, half:]).astype(BF16)
+            y_even = mm(mixed[k, 0], r_even)
+            y_odd = mm(mixed[k, 1], r_odd)
             for parity, table in enumerate((l_even, l_odd)):
                 if parity == 0:
                     a = y_even[:half] + y_even[half:]
@@ -155,25 +181,23 @@
                     ],
                     axis=0,
                 ).astype(BF16)
-                f = mm(table, u)
-                field[k, parity] = f
-                intensity[parity] += f[:half] * f[:half] + f[half:] * f[half:]
+                field[k, parity] = mm(table, u)
 
         for parity in range(2):
-            rows_of = (0, pl.ds(parity, half, 2), slice(None))
-            measured = jnp.concatenate([pattern_lo[rows_of], pattern_hi[rows_of]], axis=1)
-            coarse = measured.astype(BF16)
-            fine = (measured - coarse.astype(F32)).astype(BF16)
-            measured = mm(coarse, spread) + mm(fine, spread)
-            ratio = 1.0 - measured * lax.rsqrt(jnp.maximum(intensity[parity], 1.0))
-            here = slice(parity * half, (parity + 1) * half)
-            for k in range(modes):
-                c_re = (field[k, parity, :half] * ratio).astype(BF16)
-                c_im = (field[k, parity, half:] * ratio).astype(BF16)
-                residual[k, 0, here, :half] = c_re[:, :half]
-                residual[k, 0, here, half:] = c_im[:, :half]
-                residual[k, 1, here, :half] = c_re[:, half:]
-                residual[k, 1, here, half:] = c_im[:, half:]
+            for start in range(0, half, chunk):
+                top = slice(start, start + chunk)
+                low = slice(half + start, half + start + chunk)
+                here = slice(parity * half + start, parity * half + start + chunk)
+                waves = [(field[k, parity, top], field[k, parity, low]) for k in range(modes)]
+                intensity = sum(re * re + im * im for re, im in waves)
+                ratio = 1.0 - measured_ref[parity, top] * lax.rsqrt(jnp.maximum(intensity, 1.0))
+                for k, (re, im) in enumerate(waves):
+                    c_re = (re * ratio).astype(BF16)
+                    c_im = (im * ratio).astype(BF16)
+                    residual[k, 0, here, :half] = c_re[:, :half]
+                    residual[k, 0, here, half:] = c_im[:, :half]
+                    residual[k, 1, here, :half] = c_re[:, half:]
+                    residual[k, 1, here, half:] = c_im[:, half:]
 
         for k in range(modes):
             g_even = mm(residual[k, 0], l_even)
@@ -191,23 +215,26 @@
                     axis=0,
                 ).astype(BF16)
                 waves.append(mm(table, v))
-            for part in range(2):
-                wave = waves[0] + waves[1] if part == 0 else waves[0] - waves[1]
-                w_re, w_im = wave[:half], wave[half:]
-                here = slice(part * half, (part + 1) * half)
-                p_re = probe_ref[0, k, here].astype(F32)
-                p_im = probe_ref[1, k, here].astype(F32)
+            field[k, 0] = waves[0] + waves[1]
+            field[k, 1] = waves[0] - waves[1]
+
+        for part in range(2):
+            for start in range(0, half, chunk):
+                top = slice(start, start + chunk)
+                low = slice(half + start, half + start + chunk)
+                here = slice(part * half + start, part * half + start + chunk)
                 o_re, o_im = patch[0, here], patch[1, here]
-                t_re = p_re * w_re + p_im * w_im
-                t_im = p_re * w_im - p_im * w_re
-                if k == 0:
-                    term[0, here] = t_re
-                    term[1, here] = t_im
-                else:
-                    term[0, here] += t_re
-                    term[1, here] += t_im
-                update_ref[0, k, here] += o_re * w_re + o_im * w_im
-                update_ref[1, k, here] += o_re * w_im - o_im * w_re
+                t_re = t_im = 0.0
+                for k in range(modes):
+                    w_re, w_im = field[k, part, top], field[k, part, low]
+                    p_re = probe_ref[0, k, here].astype(F32)
+                    p_im = probe_ref[1, k, here].astype(F32)
+                    t_re += p_re * w_re + p_im * w_im
+                    t_im += p_re * w_im - p_im * w_re
+                    update_ref[0, k, here] += o_re * w_re + o_im * w_im
+                    update_ref[1, k, here] += o_re * w_im - o_im * w_re
+                term[0, here] = t_re
+                term[1, here] = t_im
 
         far = lane >= shift
         for part in range(2):
@@ -220,68 +247,66 @@
                 high = pieces[t] if t < width // lanes else 0.0
                 where = (part, pl.ds(row_base, tall), pl.ds(base + t * lanes, lanes))
                 totals[where] += rows_down(jnp.where(far, high, low), row_shift)
-
-    @pl.when(number == last)
-    def _():
-        copies = [
-            pltpu.make_async_copy(totals.at[:, pl.ds(0, margin), :], up_ref, sems.at[0]),
-            pltpu.make_async_copy(totals.at[:, pl.ds(margin, tile_rows), :], middle_ref, sems.at[1]),
-            pltpu.make_async_copy(
-                totals.at[:, pl.ds(margin + tile_rows, margin), :], down_ref, sems.at[2]
-            ),
-        ]
-        for copy in copies:
-            copy.start()
-        for copy in copies:
-            copy.wait()
-
-
-def gradients(rows, cols, count, object_field, left, right, top, bottom, probe, patterns, table):
+        return carried
+
+    lax.fori_loop(0, live, visit, 0)
+    copies = [
+        pltpu.make_async_copy(totals.at[:, pl.ds(0, margin), :], up_ref, sems.at[0, 0]),
+        pltpu.make_async_copy(
+            totals.at[:, pl.ds(margin + tile_rows, margin), :], down_ref, sems.at[0, 1]
+        ),
+        pltpu.make_async_copy(update_ref, update_out, sems.at[0, 2]),
+    ] + [
+        pltpu.make_async_copy(
+            totals.at[part, pl.ds(margin, tile_rows), :], middle_ref.at[part], sems.at[1, part]
+        )
+        for part in range(2)
+    ]
+    for copy in copies:
+        copy.start()
+    for copy in copies:
+        copy.wait()
+
+
+def gradients(offsets, counts, extended, probe, patterns, table):
     slots, width = patterns.shape[:2]
     modes = probe.shape[1]
-    tile_rows, tile_cols = object_field.shape[1:]
     margin = width // 2
-    full = (2, tile_rows + 2 * margin, tile_cols + 2 * margin)
+    full = extended.shape
+    tile_rows = full[1] - 2 * margin
     anywhere = pl.BlockSpec(memory_space=pl.ANY)
-
-    def whole(shape):
-        return pl.BlockSpec(shape, lambda n, *_: (0,) * len(shape))
-
+    scalars = pl.BlockSpec(memory_space=pltpu.SMEM)
     flops = slots * modes * 8 * 2 * width**3
     return pl.pallas_call(
         kernel,
-        grid_spec=pltpu.PrefetchScalarGridSpec(
-            num_scalar_prefetch=3,
-            grid=(slots,),
-            in_specs=[anywhere] * 5
-            + [
-                whole(probe.shape),
-                pl.BlockSpec((1, width, width // 2), lambda n, *_: (n, 0, 0)),
-                pl.BlockSpec((1, width, width // 2), lambda n, *_: (n, 0, 1)),
-                whole(table.shape),
-            ],
-            out_specs=[anywhere] * 3 + [whole(probe.shape)],
-            scratch_shapes=[
-                pltpu.VMEM(full, F32),
-                pltpu.VMEM(full, F32),
-                pltpu.VMEM((2, width, width), F32),
-                pltpu.VMEM((modes, 2, width, width), F32),
-                pltpu.VMEM((modes, 2, width, width), BF16),
-                pltpu.VMEM((2, width, width), F32),
-                pltpu.SemaphoreType.DMA((5,)),
-            ],
-        ),
+        in_specs=[scalars] * 2 + [anywhere] * 4,
+        out_specs=[anywhere] * 4,
+        scratch_shapes=[
+            pltpu.VMEM((2, 2, width + SUB, width + LANES), F32),
+            pltpu.VMEM((2, 2, width, width // 2), F32),
+            pltpu.VMEM(probe.shape, BF16),
+            pltpu.VMEM(table.shape, BF16),
+            pltpu.VMEM(full, F32),
+            pltpu.VMEM(probe.shape, F32),
+            pltpu.VMEM((2, width, width), F32),
+            pltpu.VMEM((modes, 2, width, width), BF16),
+            pltpu.VMEM((modes, 2, width, width), F32),
+            pltpu.VMEM((modes, 2, width, width), BF16),
+            pltpu.VMEM((2, width // 2, width), F32),
+            pltpu.VMEM((2, width, width), F32),
+            pltpu.SemaphoreType.DMA((3, 3)),
+        ],
         out_shape=[
             jax.ShapeDtypeStruct((2, margin, full[2]), F32),
             jax.ShapeDtypeStruct((2, tile_rows, full[2]), F32),
             jax.ShapeDtypeStruct((2, margin, full[2]), F32),
             jax.ShapeDtypeStruct(probe.shape, F32),
         ],
-        compiler_params=pltpu.CompilerParams(vmem_limit_bytes=56 * 2**20),
+        compiler_params=pltpu.CompilerParams(vmem_limit_bytes=60 * 2**20),
         cost_estimate=pl.CostEstimate(
             flops=flops, bytes_accessed=16 * 2**20, transcendentals=slots * width * width
         ),
-    )(rows, cols, count, object_field, left, right, top, bottom, probe, patterns, patterns, table)
+    )(offsets, counts, extended, probe, patterns, table)
 
 
 class Move:
@@ -345,73 +370,82 @@
         pl.semaphore_wait(barrier, peers + len(others))
 
 
-def halo_kernel(object_ref, left_ref, right_ref, top_ref, bottom_ref, send_sems, recv_sems):
+def halo_kernel(object_ref, out_ref, send_sems, recv_sems, local_sem):
     me = Place()
     tile_rows, tile_cols = object_ref.shape[1:]
-    margin = top_ref.shape[1]
+    margin = (out_ref.shape[1] - tile_rows) // 2
     sems = (send_sems, recv_sems)
-    head, tail = pl.ds(0, margin), pl.ds(tile_rows - margin, margin)
-    bands = [head, tail]
+    body, centre = pl.ds(margin, tile_rows), pl.ds(margin, tile_cols)
+    own = pltpu.make_async_copy(object_ref, out_ref.at[:, body, centre], local_sem)
+    bands = [(0, margin), (tile_rows - margin, margin)]
     if tile_rows > 2 * margin:
-        bands.append(pl.ds(margin, tile_rows - 2 * margin))
+        bands.append((margin, tile_rows - 2 * margin))
     first, final = pl.ds(0, margin), pl.ds(tile_cols - margin, margin)
-    centre = pl.ds(margin, tile_cols)
     beyond = pl.ds(margin + tile_cols, margin)
+    above, below = pl.ds(0, margin), pl.ds(margin + tile_rows, margin)
     me.greet()
     count = iter(range(send_sems.shape[0]))
 
     sides = []
-    for band in bands:
+    for start, rows in bands:
+        band, there = pl.ds(start, rows), pl.ds(margin + start, rows)
         sides.append(
             (
-                Move(object_ref.at[:, band, final], left_ref.at[:, band, :], sems, next(count),
-                     me.right, me.has_right, me.has_left),
-                Move(object_ref.at[:, band, first], right_ref.at[:, band, :], sems, next(count),
-                     me.left, me.has_left, me.has_right),
+                Move(object_ref.at[:, band, final], out_ref.at[:, there, first], sems,
+                     next(count), me.right, me.has_right, me.has_left),
+                Move(object_ref.at[:, band, first], out_ref.at[:, there, beyond], sems,
+                     next(count), me.left, me.has_left, me.has_right),
             )
         )
-    below = Move(object_ref.at[:, tail, :], top_ref.at[:, :, centre], sems, next(count),
-                 me.down, me.has_down, me.has_up)
-    above = Move(object_ref.at[:, head, :], bottom_ref.at[:, :, centre], sems, next(count),
-                 me.up, me.has_up, me.has_down)
-    moves = [move for pair in sides for move in pair] + [below, above]
+    strips = [
+        Move(object_ref.at[:, pl.ds(tile_rows - margin, margin), :], out_ref.at[:, above, centre],
+             sems, next(count), me.down, me.has_down, me.has_up),
+        Move(object_ref.at[:, pl.ds(0, margin), :], out_ref.at[:, below, centre],
+             sems, next(count), me.up, me.has_up, me.has_down),
+    ]
+    moves = [move for pair in sides for move in pair] + strips
     for move in moves:
         move.start()
+    own.start()
     corners = []
-    for number, (band, target, sends, lands, out_ref) in enumerate(
+    for number, (band, target, sends, lands, rows) in enumerate(
         [
-            (head, me.up, me.has_up, me.has_down, bottom_ref),
-            (tail, me.down, me.has_down, me.has_up, top_ref),
+            (pl.ds(margin, margin), me.up, me.has_up, me.has_down, below),
+            (pl.ds(tile_rows, margin), me.down, me.has_down, me.has_up, above),
         ]
     ):
-        for side, (src_ref, there, has) in enumerate(
-            [(left_ref, first, me.has_left), (right_ref, beyond, me.has_right)]
-        ):
+        for side, (cols, has) in enumerate([(first, me.has_left), (beyond, me.has_right)]):
             sides[number][side].arrive()
-            move = Move(src_ref.at[:, band, :], out_ref.at[:, :, there], sems, next(count),
+            move = Move(out_ref.at[:, band, cols], out_ref.at[:, rows, cols], sems, next(count),
                         target, jnp.logical_and(sends, has), jnp.logical_and(lands, has))
             move.start()
             corners.append(move)
     for pair in sides[2:]:
         for move in pair:
             move.arrive()
-    for move in [below, above] + corners:
+    for move in strips + corners:
         move.arrive()
     for move in moves + corners:
         move.leave()
+    own.wait()
 
 
 def halo(object_field, margin):
     tile_rows, tile_cols = object_field.shape[1:]
-    side = jax.ShapeDtypeStruct((2, tile_rows, margin), F32)
-    edge = jax.ShapeDtypeStruct((2, margin, tile_cols + 2 * margin), F32)
+    anywhere = pl.BlockSpec(memory_space=pl.ANY)
     return pl.pallas_call(
         halo_kernel,
-        in_specs=[pl.BlockSpec(memory_space=pl.ANY)],
-        out_specs=[pl.BlockSpec(memory_space=pl.ANY)] * 4,
-        out_shape=[side, side, edge, edge],
-        scratch_shapes=[pltpu.SemaphoreType.DMA((12,)), pltpu.SemaphoreType.DMA((12,))],
-        compiler_params=pltpu.CompilerParams(collective_id=0, has_side_effects=True),
+        in_specs=[anywhere],
+        out_specs=anywhere,
+        out_shape=jax.ShapeDtypeStruct((2, tile_rows + 2 * margin, tile_cols + 2 * margin), F32),
+        scratch_shapes=[
+            pltpu.SemaphoreType.DMA((12,)),
+            pltpu.SemaphoreType.DMA((12,)),
+            pltpu.SemaphoreType.DMA,
+        ],
+        compiler_params=pltpu.CompilerParams(
+            collective_id=0, has_side_effects=True, vmem_limit_bytes=60 * 2**20
+        ),
     )(object_field)
 
 
@@ -472,9 +506,6 @@
                      me.up, me.has_up, me.has_down),
             )
         )
-    for pair in corners:
-        for move in pair:
-            move.start()
 
     size = update_ref.shape[0]
     bases = [[0], [0]]
@@ -516,6 +547,9 @@
     current = [halving(stream, 0) for stream in streams]
     for move in current:
         move.start()
+    for pair in corners:
+        for move in pair:
+            move.start()
 
     flats = []
     if tile_rows > 2 * margin:
@@ -526,12 +560,6 @@
             Move(middle_ref.at[:, inner, first], from_right.at[:, inner, :], sems, next(count),
                  me.left, me.has_left, me.has_right),
         ]
-    flats += [
-        Move(down_ref.at[:, :, centre], above.at[:, :, centre], sems, next(count),
-             me.down, me.has_down, me.has_up),
-        Move(up_ref.at[:, :, centre], below.at[:, :, centre], sems, next(count),
-             me.up, me.has_up, me.has_down),
-    ]
     for move in flats:
         move.start()
     for copy in local:
@@ -573,6 +601,16 @@
             current[stream].start()
         if step == 0:
             send_ends()
+        if step == len(row_bits) - 1:
+            strips = [
+                Move(down_ref.at[:, :, centre], above.at[:, :, centre], sems, next(count),
+                     me.down, me.has_down, me.has_up),
+                Move(up_ref.at[:, :, centre], below.at[:, :, centre], sems, next(count),
+                     me.up, me.has_up, me.has_down),
+            ]
+            for move in strips:
+                move.start()
+            flats += strips
     for step in range(steps - 1, -1, -1):
         for stream in streams:
             move = current[stream]
@@ -636,24 +674,17 @@
             pltpu.SemaphoreType.DMA((6,)),
         ],
         compiler_params=pltpu.CompilerParams(
-            collective_id=1, has_side_effects=True, vmem_limit_bytes=40 * 2**20
+            collective_id=1, has_side_effects=True, vmem_limit_bytes=60 * 2**20
         ),
     )(up, middle, down, flat)
     return object_grad, probe_grad.reshape(update.shape)
 
 
 def on_device(object_field, probe, patterns, offsets, counts):
-    tile_rows, tile_cols = object_field.shape[1:]
     width = patterns.shape[1]
-    margin = width // 2
-    base_row = lax.axis_index("row") * tile_rows - margin
-    base_col = lax.axis_index("col") * tile_cols - margin
     table = jnp.asarray(tables(width))
-    left, right, top, bottom = halo(object_field, margin)
-    up, middle, down, update = gradients(
-        offsets[0] - base_row, offsets[1] - base_col, counts.reshape(-1),
-        object_field, left, right, top, bottom, probe, patterns, table,
-    )
+    extended = halo(object_field, width // 2)
+    up, middle, down, update = gradients(offsets, counts, extended, probe, patterns, table)
     return finish(up, middle, down, update)
 
 

time: 125 us -> 157 us (1.26)
  the two profiles are of different devices: /device:TPU:11 before, /device:TPU:0 now
where the time goes in v3:
time: 157 us
  Pallas kernels  151 us (96%)
  local copies, waits for them, and re-layouts  4.55 us (3%)
    pallas_call x1, Pallas kernels, finish(): pl.pallas_call(last_kernel, in_specs=[pl.BlockSpec(memory_space=pl.ANY)]...  73.8 us
    pallas_call x1, Pallas kernels, halo(): pl.pallas_call(halo_kernel, in_specs=[anywhere], out_specs=anywhere, out_...  67.9 us
    pallas_call x1, Pallas kernels, gradients(): pl.pallas_call(kernel, in_specs=[scalars] * 2 + [anywhere] * 4, out_specs...  9.09 us
    unnamed x4, local copies, waits for them, and re-layouts  4.55 us

profile of v3, /device:TPU:0, one launch (start us, length us, event | category | flops | bytes accessed | tf_op | source)
XLA Modules:
  0.0 156.7 jit_solution(12470487071949621327)
XLA Ops:
  1.3 67.9 %shard_map.77.extended_ref = f32[2,768,768]{2,1,0:T(8,128)} custom-call(f32[2,512,512]{2,1,0:T(8,128)} %object_ref.1), custom_call_target="tpu_custom_call" | custom-call | tf_op jit(solution)/shard_map/pallas_call | solution.py:436
  69.2 9.1 %shard_map.78 = (f32[2,128,768]{2,1,0:T(8,128)}, f32[2,512,768]{2,1,0:T(8,128)}, f32[2,128,768]{2,1,0:T(8,128)}, f32[2,4,256,256]{3,2,1,0:T(8,128)}) custom-call(s32[2,8]{1,0:T(2,128)} %offsets_ref.1, s32[1,1]{1,0:T(1,128)S(6)} %copy.10.count_ref, f32[2,768,768]{2,1,0:T(8,128)} %shard_map.77.extended_ref, bf16[2,4,256,256]{3,2,1,0:T(8,128)(2,1)} %probe_hbm.1, ...), custom_call_target="tpu_custom_call" | custom-call | flops 8589934592 | bytes 16777216 | tf_op jit(solution)/shard_map/pallas_call | solution.py:280
  78.3 73.8 %shard_map.79 = (f32[2,512,512]{2,1,0:T(8,128)}, f32[2048,256]{1,0:T(8,128)}) custom-call(f32[2,128,768]{2,1,0:T(8,128)} %get-tuple-element.8.up_ref, f32[2,512,768]{2,1,0:T(8,128)} %get-tuple-element.9.middle_ref, f32[2,128,768]{2,1,0:T(8,128)} %get-tuple-element.10.down_ref, f32[2048,256]{1,0:T(8,128)} %bitcast.2), custom_call_target="tpu_custom_call" | custom-call | tf_op jit(solution)/shard_map/pallas_call | solution.py:654
  152.1 0.0 copy-start
  152.1 3.2 %copy.11 = f32[2,512,512]{2,1,0:T(8,128)} copy(f32[2,512,512]{2,1,0:T(8,128)} %get-tuple-element.16) | data formatting | bytes 4194304
  155.4 0.0 copy-done
  155.4 1.3 copy.12
Async XLA Ops:
  152.1 3.2 %copy-start = (f32[2048,256]{1,0:T(8,128)S(1)}, f32[2048,256]{1,0:T(8,128)}, u32[]{:S(2)}) copy-start(f32[2048,256]{1,0:T(8,128)} %get-tuple-element.13) | copy-start | bytes 6291460

commit v4 on v3

--- a/solution.py
+++ b/solution.py
@@ -370,64 +370,97 @@
         pl.semaphore_wait(barrier, peers + len(others))
 
 
-def halo_kernel(object_ref, out_ref, send_sems, recv_sems, local_sem):
+def halo_kernel(object_ref, out_ref, ext, send_sems, recv_sems, local_sems):
     me = Place()
     tile_rows, tile_cols = object_ref.shape[1:]
     margin = (out_ref.shape[1] - tile_rows) // 2
     sems = (send_sems, recv_sems)
     body, centre = pl.ds(margin, tile_rows), pl.ds(margin, tile_cols)
-    own = pltpu.make_async_copy(object_ref, out_ref.at[:, body, centre], local_sem)
-    bands = [(0, margin), (tile_rows - margin, margin)]
+    first, beyond = pl.ds(0, margin), pl.ds(margin + tile_cols, margin)
+    above, below = pl.ds(0, margin), pl.ds(margin + tile_rows, margin)
+    left, right = pl.ds(margin, margin), pl.ds(tile_cols, margin)
+    bands = [(margin, margin), (tile_rows, margin)]
     if tile_rows > 2 * margin:
-        bands.append((margin, tile_rows - 2 * margin))
-    first, final = pl.ds(0, margin), pl.ds(tile_cols - margin, margin)
-    beyond = pl.ds(margin + tile_cols, margin)
-    above, below = pl.ds(0, margin), pl.ds(margin + tile_rows, margin)
+        bands.append((2 * margin, tile_rows - 2 * margin))
+    loads = [
+        pltpu.make_async_copy(
+            object_ref.at[:, pl.ds(start - margin, rows), :],
+            ext.at[:, pl.ds(start, rows), centre],
+            local_sems.at[number],
+        )
+        for number, (start, rows) in enumerate(bands)
+    ]
+    for load in loads:
+        load.start()
     me.greet()
     count = iter(range(send_sems.shape[0]))
 
     sides = []
-    for start, rows in bands:
-        band, there = pl.ds(start, rows), pl.ds(margin + start, rows)
-        sides.append(
-            (
-                Move(object_ref.at[:, band, final], out_ref.at[:, there, first], sems,
-                     next(count), me.right, me.has_right, me.has_left),
-                Move(object_ref.at[:, band, first], out_ref.at[:, there, beyond], sems,
-                     next(count), me.left, me.has_left, me.has_right),
-            )
-        )
-    strips = [
-        Move(object_ref.at[:, pl.ds(tile_rows - margin, margin), :], out_ref.at[:, above, centre],
-             sems, next(count), me.down, me.has_down, me.has_up),
-        Move(object_ref.at[:, pl.ds(0, margin), :], out_ref.at[:, below, centre],
-             sems, next(count), me.up, me.has_up, me.has_down),
+    strips = []
+    for number, (start, rows) in enumerate(bands):
+        band = pl.ds(start, rows)
+        loads[number].wait()
+        pair = (
+            Move(ext.at[:, band, right], ext.at[:, band, first], sems, next(count),
+                 me.right, me.has_right, me.has_left),
+            Move(ext.at[:, band, left], ext.at[:, band, beyond], sems, next(count),
+                 me.left, me.has_left, me.has_right),
+        )
+        sides.append(pair)
+        if number == 0:
+            strips.append(
+                Move(ext.at[:, band, centre], ext.at[:, below, centre], sems, next(count),
+                     me.up, me.has_up, me.has_down)
+            )
+        if number == 1:
+            strips.append(
+                Move(ext.at[:, band, centre], ext.at[:, above, centre], sems, next(count),
+                     me.down, me.has_down, me.has_up)
+            )
+        for move in pair:
+            move.start()
+        if number < 2:
+            strips[number].start()
+    stores = [
+        pltpu.make_async_copy(
+            ext.at[:, body, centre], out_ref.at[:, body, centre], local_sems.at[3]
+        )
     ]
-    moves = [move for pair in sides for move in pair] + strips
-    for move in moves:
-        move.start()
-    own.start()
+    stores[0].start()
     corners = []
-    for number, (band, target, sends, lands, rows) in enumerate(
-        [
-            (pl.ds(margin, margin), me.up, me.has_up, me.has_down, below),
-            (pl.ds(tile_rows, margin), me.down, me.has_down, me.has_up, above),
-        ]
+    for number, (target, sends, lands, rows) in enumerate(
+        [(me.up, me.has_up, me.has_down, below), (me.down, me.has_down, me.has_up, above)]
     ):
+        band = pl.ds(*bands[number])
         for side, (cols, has) in enumerate([(first, me.has_left), (beyond, me.has_right)]):
             sides[number][side].arrive()
-            move = Move(out_ref.at[:, band, cols], out_ref.at[:, rows, cols], sems, next(count),
+            move = Move(ext.at[:, band, cols], ext.at[:, rows, cols], sems, next(count),
                         target, jnp.logical_and(sends, has), jnp.logical_and(lands, has))
             move.start()
             corners.append(move)
     for pair in sides[2:]:
         for move in pair:
             move.arrive()
+    for number, cols in enumerate((first, beyond)):
+        stores.append(
+            pltpu.make_async_copy(
+                ext.at[:, body, cols], out_ref.at[:, body, cols], local_sems.at[4 + number]
+            )
+        )
+        stores[-1].start()
     for move in strips + corners:
         move.arrive()
-    for move in moves + corners:
+    for number, rows in enumerate((above, below)):
+        stores.append(
+            pltpu.make_async_copy(
+                ext.at[:, rows, :], out_ref.at[:, rows, :], local_sems.at[6 + number]
+            )
+        )
+        stores[-1].start()
+    for move in [move for pair in sides for move in pair] + strips + corners:
         move.leave()
-    own.wait()
+    for store in stores:
+        store.wait()
 
 
 def halo(object_field, margin):
@@ -439,9 +472,10 @@
         out_specs=anywhere,
         out_shape=jax.ShapeDtypeStruct((2, tile_rows + 2 * margin, tile_cols + 2 * margin), F32),
         scratch_shapes=[
+            pltpu.VMEM((2, tile_rows + 2 * margin, tile_cols + 2 * margin), F32),
             pltpu.SemaphoreType.DMA((12,)),
             pltpu.SemaphoreType.DMA((12,)),
-            pltpu.SemaphoreType.DMA,
+            pltpu.SemaphoreType.DMA((8,)),
         ],
         compiler_params=pltpu.CompilerParams(
             collective_id=0, has_side_effects=True, vmem_limit_bytes=60 * 2**20
@@ -454,9 +488,9 @@
 
 
 def last_kernel(
-    up_ref, middle_ref, down_ref, update_ref,
+    up_hbm, middle_ref, down_hbm, update_ref,
     object_ref, probe_ref,
-    above, below, from_left, from_right, edges, total, landed,
+    up_ref, down_ref, above, below, from_left, from_right, edges, total, landed,
     send_sems, recv_sems, sum_send, sum_recv, local_sems,
 ):
     me = Place()
@@ -480,17 +514,12 @@
 
     local = [
         pltpu.make_async_copy(update_ref, total, local_sems.at[0]),
-        pltpu.make_async_copy(middle_ref.at[:, :, centre], object_ref, local_sems.at[1]),
+        pltpu.make_async_copy(up_hbm, up_ref, local_sems.at[1]),
+        pltpu.make_async_copy(down_hbm, down_ref, local_sems.at[2]),
+        pltpu.make_async_copy(middle_ref.at[:, :, first], edges.at[0], local_sems.at[3]),
+        pltpu.make_async_copy(middle_ref.at[:, :, beyond], edges.at[1], local_sems.at[4]),
+        pltpu.make_async_copy(middle_ref.at[:, :, centre], object_ref, local_sems.at[5]),
     ]
-    for side, cols in enumerate((first, beyond)):
-        for end, band in enumerate((head, tail)):
-            local.append(
-                pltpu.make_async_copy(
-                    middle_ref.at[:, band, cols],
-                    edges.at[side, end],
-                    local_sems.at[2 + 2 * side + end],
-                )
-            )
     for copy in local:
         copy.start()
     me.greet([partner(axis, bit) for axis, bit in orders[0] if bit > 1])
@@ -519,9 +548,8 @@
         keep = pl.multiple_of(base + half * rows, SUB)
         give = pl.multiple_of(base + (1 - half) * rows, SUB)
         bases[stream].append(keep)
-        source = update_ref if step == 0 else total
         return Move(
-            source.at[pl.ds(give, rows), lanes],
+            total.at[pl.ds(give, rows), lanes],
             landed.at[pl.ds(size - 2 * rows, rows), lanes],
             (sum_send.at[stream], sum_recv.at[stream]), step, partner(axis, bit),
         )
@@ -545,26 +573,28 @@
     streams = range(2)
     sums = []
     current = [halving(stream, 0) for stream in streams]
+    local[0].wait()
     for move in current:
         move.start()
+    local[1].wait()
+    local[2].wait()
     for pair in corners:
         for move in pair:
             move.start()
+    local[3].wait()
+    local[4].wait()
 
     flats = []
     if tile_rows > 2 * margin:
         inner = pl.ds(margin, tile_rows - 2 * margin)
         flats = [
-            Move(middle_ref.at[:, inner, beyond], from_left.at[:, inner, :], sems, next(count),
+            Move(edges.at[1, :, inner, :], from_left.at[:, inner, :], sems, next(count),
                  me.right, me.has_right, me.has_left),
-            Move(middle_ref.at[:, inner, first], from_right.at[:, inner, :], sems, next(count),
+            Move(edges.at[0, :, inner, :], from_right.at[:, inner, :], sems, next(count),
                  me.left, me.has_left, me.has_right),
         ]
     for move in flats:
         move.start()
-    for copy in local:
-        copy.wait()
-
     ends = []
 
     def send_ends():
@@ -579,11 +609,11 @@
             ):
                 corners[side][end].arrive()
 
-                def add(side=side, end=end, got=got, cols=cols):
-                    edges[side, end] += got[:, :, cols]
+                def add(side=side, band=band, got=got, cols=cols):
+                    edges[side, :, band, :] += got[:, :, cols]
 
                 when(has, add)
-                move = Move(edges.at[side, end], out_ref.at[:, band, :], sems, next(count),
+                move = Move(edges.at[side, :, band, :], out_ref.at[:, band, :], sems, next(count),
                             target, sends, lands)
                 move.start()
                 ends.append(move)
@@ -620,6 +650,7 @@
                 current[stream] = doubling(stream, step - 1)
                 current[stream].start()
 
+    local[5].wait()
     for move in flats + ends:
         move.arrive()
 
@@ -662,9 +693,11 @@
         scratch_shapes=[
             pltpu.VMEM(up.shape, F32),
             pltpu.VMEM(up.shape, F32),
+            pltpu.VMEM(up.shape, F32),
+            pltpu.VMEM(up.shape, F32),
             pltpu.VMEM((2, tile_rows, margin), F32),
             pltpu.VMEM((2, tile_rows, margin), F32),
-            pltpu.VMEM((2, 2, 2, margin, margin), F32),
+            pltpu.VMEM((2, 2, tile_rows, margin), F32),
             pltpu.VMEM(flat.shape, F32),
             pltpu.VMEM(flat.shape, F32),
             pltpu.SemaphoreType.DMA((12,)),

time: 157 us -> 111 us (0.71)
  Pallas kernels: 151 us -> 105 us
    pallas_call x1, Pallas kernels: 67.9 us -> 18.6 us  [halo(): pl.pallas_call(halo_kernel, in_specs=[anywhere], out_specs=anywhere, out_...]
    pallas_call x1, Pallas kernels: 9.09 us -> 16.5 us  [gradients(): pl.pallas_call(kernel, in_specs=[scalars] * 2 + [anywhere] * 4, out_specs...]
    pallas_call x1, Pallas kernels: 73.8 us -> 69.7 us  [finish(): pl.pallas_call(last_kernel, in_specs=[pl.BlockSpec(memory_space=pl.ANY)]...]
where the time goes in v4:
time: 111 us
  Pallas kernels  105 us (95%)
  local copies, waits for them, and re-layouts  4.55 us (4%)
  between operations  1.31 us (1%)
    pallas_call x1, Pallas kernels, finish(): pl.pallas_call(last_kernel, in_specs=[pl.BlockSpec(memory_space=pl.ANY)]...  69.7 us
    pallas_call x1, Pallas kernels, halo(): pl.pallas_call(halo_kernel, in_specs=[anywhere], out_specs=anywhere, out_...  18.6 us
    pallas_call x1, Pallas kernels, gradients(): pl.pallas_call(kernel, in_specs=[scalars] * 2 + [anywhere] * 4, out_specs...  16.5 us
    unnamed x4, local copies, waits for them, and re-layouts  4.55 us

profile of v4, /device:TPU:0, one launch (start us, length us, event | category | flops | bytes accessed | tf_op | source)
XLA Modules:
  0.0 110.6 jit_solution(14461442150450091228)
XLA Ops:
  1.3 18.6 %shard_map.77.extended_ref = f32[2,768,768]{2,1,0:T(8,128)} custom-call(f32[2,512,512]{2,1,0:T(8,128)} %object_ref.1), custom_call_target="tpu_custom_call" | custom-call | tf_op jit(solution)/shard_map/pallas_call | solution.py:469
  19.9 16.5 %shard_map.78 = (f32[2,128,768]{2,1,0:T(8,128)}, f32[2,512,768]{2,1,0:T(8,128)}, f32[2,128,768]{2,1,0:T(8,128)}, f32[2,4,256,256]{3,2,1,0:T(8,128)}) custom-call(s32[2,8]{1,0:T(2,128)} %offsets_ref.1, s32[1,1]{1,0:T(1,128)S(6)} %copy.10.count_ref, f32[2,768,768]{2,1,0:T(8,128)} %shard_map.77.extended_ref, bf16[2,4,256,256]{3,2,1,0:T(8,128)(2,1)} %probe_hbm.1, ...), custom_call_target="tpu_custom_call" | custom-call | flops 8589934592 | bytes 16777216 | tf_op jit(solution)/shard_map/pallas_call | solution.py:280
  36.4 69.7 %shard_map.79 = (f32[2,512,512]{2,1,0:T(8,128)}, f32[2048,256]{1,0:T(8,128)}) custom-call(f32[2,128,768]{2,1,0:T(8,128)} %get-tuple-element.8.up_hbm, f32[2,512,768]{2,1,0:T(8,128)} %get-tuple-element.9.middle_ref, f32[2,128,768]{2,1,0:T(8,128)} %get-tuple-element.10.down_hbm, f32[2048,256]{1,0:T(8,128)} %bitcast.2), custom_call_target="tpu_custom_call" | custom-call | tf_op jit(solution)/shard_map/pallas_call | solution.py:685
  106.1 0.0 copy-start
  106.1 3.2 %copy.11 = f32[2,512,512]{2,1,0:T(8,128)} copy(f32[2,512,512]{2,1,0:T(8,128)} %get-tuple-element.16) | data formatting | bytes 4194304
  109.3 0.0 copy-done
  109.3 1.3 %copy.12 = f32[2,4,256,256]{3,2,1,0:T(8,128)} copy(f32[2,4,256,256]{3,2,1,0:T(8,128)S(1)} %bitcast.3) | data formatting | bytes 4194304
Async XLA Ops:
  106.1 3.2 %copy-start = (f32[2048,256]{1,0:T(8,128)S(1)}, f32[2048,256]{1,0:T(8,128)}, u32[]{:S(2)}) copy-start(f32[2048,256]{1,0:T(8,128)} %get-tuple-element.13) | copy-start | bytes 6291460
